TPU v7x, 128 devices: a whole 4x4x4 slice. The times are simulated.
128 devices in a mesh: section: 8 (over y, core), dp: 16 (over x, z).
Axes of the slice: x: 4, y: 4, z: 4, core: 2. Of those that a mesh axis runs over, the one named last changes fastest.
Arguments:
- old_slot: int32 [24], replicated, may hold values from 0 to 23, as said below
- new_slot: int32 [24], replicated, may hold values from 0 to 23, as said below
- a_old: bfloat16 [24, 64, 16384], P('section', None, 'dp'), may hold values from -0.046875 to 0.046875
- a_first_old: float32 [24, 64, 16384], P('section', None, 'dp'), may hold values from -3 to 3
- a_second_old: float32 [24, 64, 16384], P('section', None, 'dp'), may hold values from 0.01 to 1
- b_old: bfloat16 [24, 64, 1024], P('section', None, 'dp'), may hold values from -0.75 to 0.75
- b_first_old: float32 [24, 64, 1024], P('section', None, 'dp'), may hold values from -0.75 to 0.75
- b_second_old: float32 [24, 64, 1024], P('section', None, 'dp'), may hold values from 0.005 to 0.5
- inputs: bfloat16 [16, 4096, 16384], P('section', 'dp'), may hold values from -6 to 6
- cotangent: bfloat16 [16, 4096, 1024], P('section', 'dp'), may hold values from -0.005859375 to 0.005859375
Outputs:
- adapter_out: bfloat16 [16, 4096, 1024], P('section', 'dp')
- new_a: bfloat16 [32, 64, 16384], P('section', None, 'dp')
- new_b: bfloat16 [32, 64, 1024], P('section', None, 'dp')
- a_first_new: float32 [32, 64, 16384], P('section', None, 'dp')
- a_second_new: float32 [32, 64, 16384], P('section', None, 'dp')
- b_first_new: float32 [32, 64, 1024], P('section', None, 'dp')
- b_second_new: float32 [32, 64, 1024], P('section', None, 'dp')
- a_step: float32 [16, 64, 16384], P('section', None, 'dp')
- b_step: float32 [16, 64, 1024], P('section', None, 'dp')
Inputs may be any that keep to these rules, and one draw needn't show every extreme that they name: `old_slot`: A permutation of the old slots; old slot i lies on section i // 3, so every old slot holds a layer. `new_slot`: distinct values filling every slot of the first 6 sections (new slot i lies on section i // 4); the last sections hold no layer; no two layers that share an old section share a new section.
All inputs are finite; a program needn't handle non-finite values.
Results may differ from a plain program's by a relative error of at most 0.0049.
Values may be sent and summed in bfloat16 or wider, within the bound.
A program may use at most 128 MiB of HBM per device.

v0:
```python
import jax
import jax.numpy as jnp
from jax import lax
from jax.sharding import PartitionSpec as P

NEW_DEV = 4
WIN = 2


adapter_scale = 2.0
beta_one = 0.9
beta_two = 0.999
adam_eps = 1e-08
corr_one = 1.0 - (0.9**10) ** 10
corr_two = 1.0 - (0.999**10) ** 10


def adam_update(first, second, grad):
    first_new = beta_one * first + (1.0 - beta_one) * grad
    second_new = beta_two * second + (1.0 - beta_two) * grad * grad
    direction = first_new / corr_one / (jnp.sqrt(second_new / corr_two) + adam_eps)
    return (first_new, second_new, direction)


def select_rows(array, index, flag):
    picked = jnp.take(array, index, axis=0)
    array_shape = flag.shape + (1,) * (array.ndim - 1)
    return jnp.where(flag.reshape(array_shape), picked, jnp.zeros_like(picked))


def route_tables(old_slot, new_slot, own_section, sections, old_dev):
    old_section = old_slot // old_dev
    new_section = new_slot // NEW_DEV
    local = jnp.arange(old_dev, dtype=jnp.int32)
    mine = (old_slot[:, None] == own_section * old_dev + local[None, :]).astype(jnp.int32)
    heading = jnp.sum(mine * new_section[:, None], axis=0)
    peers = jnp.arange(sections, dtype=jnp.int32)
    sending = (heading[None, :] == peers[:, None]).astype(jnp.int32)
    send_index = jnp.sum(sending * local[None, :], axis=1)
    send_has = jnp.sum(sending, axis=1) > 0
    spots = jnp.arange(NEW_DEV, dtype=jnp.int32)
    landing = (new_slot[:, None] == own_section * NEW_DEV + spots[None, :]).astype(jnp.int32)
    source = jnp.sum(landing * old_section[:, None], axis=0)
    present = jnp.sum(landing, axis=0) > 0
    return (send_index, send_has, source, present)


def body(
    old_slot,
    new_slot,
    a_old,
    a_first_old,
    a_second_old,
    b_old,
    b_first_old,
    b_second_old,
    inputs,
    cotangent,
):
    sections = lax.axis_size("section")
    own_section = lax.axis_index("section")
    old_dev = a_old.shape[0]
    rank = a_old.shape[1]
    local_d = a_old.shape[2]
    local_kv = b_old.shape[2]
    extra = rank * local_kv // local_d
    factors = jnp.concatenate([a_old, b_old.reshape(old_dev, extra, local_d)], 1)
    first_rows = jnp.concatenate([a_first_old, b_first_old.reshape(old_dev, extra, local_d)], 1)
    second_rows = jnp.concatenate([a_second_old, b_second_old.reshape(old_dev, extra, local_d)], 1)
    moments = jnp.stack([first_rows, second_rows], 1)
    send_index, send_has, source, present = route_tables(
        old_slot, new_slot, own_section, sections, old_dev
    )
    landed_f = lax.all_to_all(
        select_rows(factors, send_index, send_has),
        "section",
        split_axis=0,
        concat_axis=0,
        tiled=True,
    )
    landed_m = lax.all_to_all(
        select_rows(moments, send_index, send_has),
        "section",
        split_axis=0,
        concat_axis=0,
        tiled=True,
    )
    placed_f = select_rows(landed_f, source, present)
    placed_m = select_rows(landed_m, source, present)
    new_a = placed_f[:, :rank]
    new_b = placed_f[:, rank:].reshape(NEW_DEV, rank, local_kv)
    first_a = placed_m[:, 0, :rank]
    second_a = placed_m[:, 1, :rank]
    first_b = placed_m[:, 0, rank:].reshape(NEW_DEV, rank, local_kv)
    second_b = placed_m[:, 1, rank:].reshape(NEW_DEV, rank, local_kv)
    full_a, complete_up_factor = (
        lax.all_gather(new_a[:WIN], "dp", axis=2, tiled=True),
        lax.all_gather(new_b[:WIN], "dp", axis=2, tiled=True),
    )
    low_rank_hidden = jnp.einsum(
        "wtd,wrd->wtr", inputs, full_a, preferred_element_type=jnp.float32
    ).astype(jnp.bfloat16)
    adapted_output = (
        adapter_scale
        * jnp.einsum(
            "gqf,gfl->gql", low_rank_hidden, complete_up_factor, preferred_element_type=jnp.float32
        )
    ).astype(jnp.bfloat16)
    fetched_rows = jnp.einsum(
        "wtk,wrk->wtr", cotangent, complete_up_factor, preferred_element_type=jnp.float32
    ).astype(jnp.bfloat16)
    width_kv = cotangent.shape[2]
    up_factor_term = (
        adapter_scale
        * jnp.einsum("wtr,wtk->kwr", low_rank_hidden, cotangent, preferred_element_type=jnp.float32)
    ).reshape(width_kv, -1)
    product_term = jnp.einsum(
        "wtd,wtr->dwr", inputs, fetched_rows, preferred_element_type=jnp.float32
    )
    replica = lax.axis_index("dp")
    share_a = lax.dynamic_slice_in_dim(
        lax.psum(
            (adapter_scale * product_term).reshape(inputs.shape[2], -1).astype(jnp.bfloat16), "dp"
        ).astype(jnp.float32),
        replica * local_d,
        local_d,
        0,
    )
    share_b = lax.dynamic_slice_in_dim(
        lax.psum(up_factor_term.astype(jnp.bfloat16), "dp").astype(jnp.float32),
        replica * local_kv,
        local_kv,
        0,
    )
    down_factor_gradient = share_a.reshape(local_d, WIN, rank).transpose(1, 2, 0)
    up_factor_gradient = share_b.reshape(local_kv, WIN, rank).transpose(1, 2, 0)
    upd_first_a, upd_second_a, step_a = adam_update(
        first_a[:WIN], second_a[:WIN], down_factor_gradient
    )
    upd_first_b, upd_second_b, step_b = adam_update(
        first_b[:WIN], second_b[:WIN], up_factor_gradient
    )
    first_a = jnp.concatenate([upd_first_a, first_a[WIN:]], 0)
    second_a = jnp.concatenate([upd_second_a, second_a[WIN:]], 0)
    first_b = jnp.concatenate([upd_first_b, first_b[WIN:]], 0)
    second_b = jnp.concatenate([upd_second_b, second_b[WIN:]], 0)
    return (adapted_output, new_a, new_b, first_a, second_a, first_b, second_b, step_a, step_b)


def solution(mesh):
    in_specs = (
        P(),
        P(),
        P("section", None, "dp"),
        P("section", None, "dp"),
        P("section", None, "dp"),
        P("section", None, "dp"),
        P("section", None, "dp"),
        P("section", None, "dp"),
        P("section", "dp", None),
        P("section", "dp", None),
    )
    out_specs = (
        P("section", "dp", None),
        P("section", None, "dp"),
        P("section", None, "dp"),
        P("section", None, "dp"),
        P("section", None, "dp"),
        P("section", None, "dp"),
        P("section", None, "dp"),
        P("section", None, "dp"),
        P("section", None, "dp"),
    )
    return jax.shard_map(body, mesh=mesh, in_specs=in_specs, out_specs=out_specs, check_vma=False)
```

profile of v0, /device:TPU:0, one launch (start us, length us, event | category | flops | bytes accessed | tf_op | source)
XLA Modules:
  0.0 233.2 jit_solution(16592471700938181576)
XLA Ops:
  7.2 0.7 and_select_fusion
  8.0 0.8 select_reduce_fusion.1
  8.9 0.9 reshape.124
  9.8 1.0 pad_maximum_fusion.5
  10.9 0.6 gather_fusion
  11.5 1.2 select_select_fusion.2
  12.7 4.7 %all-to-all-start = ((bf16[8,68,1024]{2,1,0:T(8,128)(2,1)}), bf16[8,68,1024]{2,1,0:T(8,128)(2,1)S(1)}, u32[]{:S(2)}, u32[]{:S(2)}) async-start(bf16[8,68,1024]{2,1,0:T(8,128)(2,1)} %select_select_fusion.2), calls=%async_computation | async-start | bytes 2359296 | tf_op jit(solution)/shard_map/all_to_all | solution.py:74
  17.5 0.2 fusion.9
  17.7 17.0 %all-to-all-done = bf16[8,68,1024]{2,1,0:T(8,128)(2,1)S(1)} async-done(((bf16[8,68,1024]{2,1,0:T(8,128)(2,1)}), bf16[8,68,1024]{2,1,0:T(8,128)(2,1)S(1)}, u32[]{:S(2)}, u32[]{:S(2)}) %all-to-all-start) | async-done | bytes 1114144 | tf_op jit(solution)/shard_map/all_to_all | solution.py:74
  34.8 1.4 gather_fusion.1
  36.2 1.2 select_select_fusion.3
  37.4 0.7 slice.94
  38.2 0.1 reshape.126
  38.3 0.1 reshape.127
  38.4 1.2 pad_maximum_fusion.4
  39.6 0.6 stack.10
  40.2 0.1 pad_maximum_fusion.3
  40.3 0.6 stack.9
  40.9 1.5 pad_maximum_fusion
  42.4 6.5 %gather_fusion.2 = f32[8,2,68,1024]{3,1,2,0:T(2,128)} fusion(f32[3,2,68,1024]{3,1,2,0:T(2,128)S(1)} %pad_maximum_fusion, s32[1024]{0:T(1024)S(1)} %pad_clamp_fusion.1), kind=kCustom, calls=%fused_computation.2 | custom fusion | bytes 8912928 | tf_op jit(solution)/shard_map/jit(_take)/gather | solution.py:26
  48.9 6.8 %select_select_fusion = f32[8,2,68,1024]{3,1,2,0:T(2,128)} fusion(f32[8,2,68,1024]{3,1,2,0:T(2,128)} %gather_fusion.2, pred[8]{0:T(512)(128)(4,1)S(1)} %get-tuple-element.29, pred[8]{0:T(512)(128)(4,1)S(1)} %get-tuple-element.30), kind=kLoop, calls=%fused_computation.6 | loop fusion | flops 2228224 | bytes 8912912 | tf_op jit(solution)/shard_map/jit(_where)/select_n | solution.py:28
  55.7 4.6 %all-to-all-start.1 = ((f32[8,2,68,1024]{3,1,2,0:T(2,128)}), f32[8,2,68,1024]{3,1,2,0:T(2,128)}, u32[]{:S(2)}, u32[]{:S(2)}) async-start(f32[8,2,68,1024]{3,1,2,0:T(2,128)} %select_select_fusion), calls=%async_computation.1 | async-start | bytes 8912896 | tf_op jit(solution)/shard_map/all_to_all | solution.py:81
  60.5 0.1 copy.31
  60.6 26.7 %all_gather.7 = bf16[2,64,1024]{1,0,2:T(2,128)(2,1)S(1)} all-gather(bf16[2,64,64]{1,0,2:T(2,128)(2,1)S(1)} %copy.31), channel_id=1, replica_groups=mesh['section'=8,'dp'=16] {'dp'}, dimensions={2}, use_global_device_ids=true | all-gather | bytes 278528 | tf_op jit(solution)/shard_map/all_gather | solution.py:98
  87.2 0.6 copy.32
  87.8 11.2 %fusion = bf16[2,64,16384]{2,1,0:T(8,128)(2,1)} fusion(bf16[2,256,16384]{2,1,0:T(8,128)(2,1)} %param.18, bf16[2,64,1024]{2,1,0:T(8,128)(2,1)S(1)} %copy.32, bf16[2,256,1024]{2,1,0:T(8,128)(2,1)S(1)} %copy-done), kind=kOutput, calls=%fused_computation.5 | convolution fusion | flops 1145077760 | bytes 22282240 | tf_op jit(solution)/shard_map/wtd,wtr->dwr/dot_general | solution.py:117
  99.0 12.2 %convolution_convert_fusion.1 = bf16[2,64,256]{2,1,0:T(8,128)(2,1)S(1)} fusion(bf16[2,64,16384]{2,1,0:T(8,128)(2,1)} %all-gather.2.cloned.1.call-done, bf16[2,256,16384]{2,1,0:T(8,128)(2,1)} %param.18), kind=kOutput, calls=%fused_computation.14 | convolution fusion | flops 1073774592 | bytes 21037056 | tf_op jit(solution)/shard_map/wtd,wrd->wtr/dot_general | solution.py:100
  111.2 1.0 fusion.1
  112.3 1.0 copy-done.2
  113.3 0.8 slice.96
  114.1 0.7 reshape.125
  114.9 5.2 %gather_fusion.3 = f32[4,2,68,1024]{3,1,2,0:T(2,128)S(1)} fusion(f32[8,2,68,1024]{3,1,2,0:T(2,128)} %all-to-all-done.1, s32[1024]{0:T(1024)S(1)} %pad_clamp_fusion), kind=kCustom, calls=%fused_computation.3 | custom fusion | bytes 4456464 | tf_op jit(solution)/shard_map/jit(_take)/gather | solution.py:26
  120.1 1.2 select_select_fusion.1
  121.3 2.4 %fusion.16 = (f32[2,1,64,1024]{3,1,2,0:T(1,128)S(1)}, f32[2,1,64,1024]{3,1,2,0:T(1,128)S(1)}, f32[2,1,64,1024]{3,1,2,0:T(1,128)S(1)}, f32[2,1,64,1024]{3,1,2,0:T(1,128)}) fusion(f32[4,2,68,1024]{3,1,2,0:T(2,128)S(1)} %select_select_fusion.1), kind=kLoop, calls=%fused_computation.72 | loop fusion | bytes 4194304 | tf_op jit(solution)/shard_map/slice | solution.py:144
  123.8 0.4 fusion.7
  124.2 0.7 mul.156
  125.0 0.7 mul.148
  125.8 0.7 slice.85
  126.6 1.4 multiply_convert_fusion
  128.1 90.1 %all-reduce.3.cloned.1.call-done = (bf16[16384,128]{0,1:T(8,128)(2,1)}, bf16[1024,128]{0,1:T(8,128)(2,1)}) async-done(((bf16[16384,128]{0,1:T(8,128)(2,1)}, bf16[1024,128]{0,1:T(8,128)(2,1)}), (bf16[16384,128]{0,1:T(8,128)(2,1)}, bf16[1024,128]{0,1:T(8,128)(2,1)})) %all-reduce.3.cloned.1.call-update) | async-done | bytes 4456464 | tf_op jit(solution)/shard_map/psum | solution.py:122
  218.2 1.0 dynamic-slice_convert_fusion
  219.2 0.8 dynamic-slice_convert_fusion.1
  220.0 0.7 add_divide_fusion.1
  220.7 0.7 pad_maximum_fusion.7
  221.4 0.7 pad_maximum_fusion.6
  222.0 2.2 add_divide_fusion
  224.3 1.0 pad_maximum_fusion.2
  225.3 1.0 pad_maximum_fusion.1
  (47 shorter events, 0.7 us)
Async XLA Ops:
  7.2 80.6 %copy-start = (bf16[2,256,1024]{2,1,0:T(8,128)(2,1)S(1)}, bf16[2,256,1024]{2,1,0:T(8,128)(2,1)}, u32[]{:S(2)}) copy-start(bf16[2,256,1024]{2,1,0:T(8,128)(2,1)} %param.19) | copy-start | bytes 3145732
  11.5 6.0 %copy-start.12 = (s32[24]{0:T(128)S(1)}, s32[24]{0:T(128)}, u32[]{:S(2)}) copy-start(s32[24]{0:T(128)} %param.10) | copy-start | bytes 292
  11.5 6.0 %copy-start.11 = (s32[24]{0:T(128)S(1)}, s32[24]{0:T(128)}, u32[]{:S(2)}) copy-start(s32[24]{0:T(128)} %param.11) | copy-start | bytes 292
  12.7 25.4 %copy-start.9 = (f32[3,64,64]{2,1,0:T(8,128)S(1)}, f32[3,64,64]{2,1,0:T(8,128)}, u32[]{:S(2)}) copy-start(f32[3,64,64]{2,1,0:T(8,128)} %param.16) | copy-start | bytes 147460
  12.7 22.1 %all-to-all-start = ((bf16[8,68,1024]{2,1,0:T(8,128)(2,1)}), bf16[8,68,1024]{2,1,0:T(8,128)(2,1)S(1)}, u32[]{:S(2)}, u32[]{:S(2)}) async-start(bf16[8,68,1024]{2,1,0:T(8,128)(2,1)} %select_select_fusion.2), calls=%async_computation | async-start | bytes 2359296 | tf_op jit(solution)/shard_map/all_to_all | solution.py:74
  17.4 20.9 %copy-start.10 = (f32[3,64,64]{2,1,0:T(8,128)S(1)}, f32[3,64,64]{2,1,0:T(8,128)}, u32[]{:S(2)}) copy-start(f32[3,64,64]{2,1,0:T(8,128)} %param.17) | copy-start | bytes 147460
  17.4 81.5 %all-gather.2.cloned.1.call-start = ((), (), s32[]{:S(2)}) async-start(), calls=%async_computation.2 | async-start | bytes 4456448 | tf_op jit(solution)/shard_map/all_gather | solution.py:97
  37.4 22.9 %copy-start.1 = (bf16[4,68,1024]{2,1,0:T(8,128)(2,1)}, bf16[4,68,1024]{2,1,0:T(8,128)(2,1)S(1)}, u32[]{:S(2)}) copy-start(bf16[4,68,1024]{2,1,0:T(8,128)(2,1)S(1)} %select_select_fusion.3) | copy-start | bytes 1671172
  37.4 2.8 %copy-start.5 = (f32[3,64,1024]{2,1,0:T(8,128)S(1)}, f32[3,64,1024]{2,1,0:T(8,128)}, u32[]{:S(2)}) copy-start(f32[3,64,1024]{2,1,0:T(8,128)} %param.13) | copy-start | bytes 2359300
  55.7 59.2 %all-to-all-start.1 = ((f32[8,2,68,1024]{3,1,2,0:T(2,128)}), f32[8,2,68,1024]{3,1,2,0:T(2,128)}, u32[]{:S(2)}, u32[]{:S(2)}) async-start(f32[8,2,68,1024]{3,1,2,0:T(2,128)} %select_select_fusion), calls=%async_computation.1 | async-start | bytes 8912896 | tf_op jit(solution)/shard_map/all_to_all | solution.py:81
  60.3 157.9 %all-reduce.3.cloned.1.call-start = ((), (), s32[]{:S(2)}) async-start(), calls=%async_computation.3 | async-start | bytes 8912896 | tf_op jit(solution)/shard_map/psum | solution.py:122
  111.2 1.0 copy-start.3
  112.2 1.1 copy-start.2
  123.7 2.8 %copy-start.4 = (bf16[2,64,256]{2,1,0:T(8,128)(2,1)S(1)}, bf16[2,64,256]{2,1,0:T(8,128)(2,1)}, u32[]{:S(2)}) copy-start(bf16[2,64,256]{2,1,0:T(8,128)(2,1)} %copy-done.3) | copy-start | bytes 196612
  126.6 93.4 %copy-start.6 = (f32[2,64,64]{2,1,0:T(8,128)S(1)}, f32[2,64,64]{2,1,0:T(8,128)}, u32[]{:S(2)}) copy-start(f32[2,64,64]{2,1,0:T(8,128)} %mul.156) | copy-start | bytes 98308
  126.6 93.4 %copy-start.7 = (f32[2,64,64]{2,1,0:T(8,128)S(1)}, f32[2,64,64]{2,1,0:T(8,128)}, u32[]{:S(2)}) copy-start(f32[2,64,64]{2,1,0:T(8,128)} %mul.148) | copy-start | bytes 98308
  126.6 94.1 %copy-start.8 = (f32[2,64,64]{2,1,0:T(8,128)S(1)}, f32[2,64,64]{2,1,0:T(8,128)}, u32[]{:S(2)}) copy-start(f32[2,64,64]{2,1,0:T(8,128)} %slice.85) | copy-start | bytes 98308
Sparse Core Ops, SparseCore 0:
  38.3 54.3 all-gather.1
  112.4 105.7 all-reduce.2
where the time goes:
time: 235 us; the launch traced here: 233 us
  waiting for transfers between devices  107 us (46%)
  blocking collectives  26.7 us (11%)
  matrix products  25.9 us (11%)
  local copies, waits for them, and re-layouts  25.1 us (11%)
  other arithmetic  24.7 us (11%)
  between operations  14.4 us (6%)
  starting transfers between devices  9.33 us (4%)
    psum x1, waiting for transfers between devices, body(): lax.psum((adapter_scale * product_term).reshape(inputs.shape[2], -1).asty...  90.1 us
    all_gather x1, blocking collectives, body(): lax.all_gather(new_b[:WIN], 'dp', axis=2, tiled=True)  26.7 us
    all_to_all x1, waiting for transfers between devices, body(): lax.all_to_all(select_rows(factors, send_index, send_has), 'section', spl...  17 us
    gather x4, local copies, waits for them, and re-layouts, select_rows(): picked = jnp.take(array, index, axis=0)  13.7 us
    dot_general x1, matrix products, body(): jnp.einsum('wtd,wrd->wtr', inputs, full_a, preferred_element_type=jnp.flo...  12.2 us
    dot_general x1, matrix products, body(): jnp.einsum('wtd,wtr->dwr', inputs, fetched_rows, preferred_element_type=j...  11.2 us
    select_n x4, other arithmetic, select_rows(): return jnp.where(flag.reshape(array_shape), picked, jnp.zeros_like(picked))  10.4 us
  transfers between devices with their start and end apart: 4, of which 2 were waited for; matrix products, arithmetic and copies ran while one was open for 25% of the time, Pallas kernels for 0%

commit v1 on v0

v1 whole, which is shorter than its diff:
```python
import jax
import jax.numpy as jnp
from jax import lax
from jax.experimental import pallas as pl
from jax.experimental.pallas import tpu as pltpu
from jax.sharding import PartitionSpec as P

MESH = pl.DeviceIdType.MESH
F32 = jnp.float32
BF16 = jnp.bfloat16

OLD_DEV = 3
NEW_DEV = 4
WIN = 2
LAYERS = 24
N_SECTION = 8
N_NEW = 6
N_DP = 16
SIDE = 4
R = 64
HALF = 32
TOK = 256
LD = 1024
LK = 64
KV = 1024

adapter_scale = 2.0
beta_one = 0.9
beta_two = 0.999
adam_eps = 1e-08
corr_one = 1.0 - (0.9**10) ** 10
corr_two = 1.0 - (0.999**10) ** 10


def dot_nt(a, b):
    return lax.dot_general(a, b, (((1,), (1,)), ((), ())), preferred_element_type=F32)


def dot_nn(a, b):
    return jnp.dot(a, b, preferred_element_type=F32)


class Messages:
    def __init__(self, send_sem, recv_sem):
        self.send_sem, self.recv_sem = send_sem, recv_sem
        self.count = 0

    def make(self, src, dst, device):
        i = self.count
        self.count += 1
        return pltpu.make_async_remote_copy(
            src_ref=src,
            dst_ref=dst,
            send_sem=self.send_sem.at[i],
            recv_sem=self.recv_sem.at[i],
            device_id=device,
            device_id_type=MESH,
        )


N_MSG = 200


def exchange_kernel(
    old_slot,
    new_slot,
    a_old,
    a_first_old,
    a_second_old,
    b_old,
    b_first_old,
    b_second_old,
    inputs,
    cotangent,
    pa_out,
    pm_out,
    pb_out,
    pbm_out,
    ga_out,
    gb_out,
    lat_out,
    bw_out,
    xin,
    cot,
    av,
    mv1,
    mv2,
    bv,
    bmv1,
    bmv2,
    b_stage,
    b_recv,
    bm_stage,
    bm_recv,
    a_stage0,
    a_stage1,
    a_recv0,
    a_recv1,
    m_stage,
    m_recv,
    afull,
    bfull,
    bw,
    pulled,
    lat_acc,
    lat,
    gb_stage,
    gb_recv,
    gsend,
    grecv,
    hbuf,
    hsend,
    hrecv,
    pa,
    pm,
    pb,
    pbm,
    ga,
    gb,
    send_sem,
    recv_sem,
    load_sem,
    x_sem,
    out_sem,
):
    me_s = lax.axis_index("section")
    me_d = lax.axis_index("dp")
    mx = me_d // SIDE
    mz = me_d % SIDE

    def at(dx, dz):
        return ((mx + dx) % SIDE) * SIDE + (mz + dz) % SIDE

    msgs = Messages(send_sem, recv_sem)

    def load(src, dst, i):
        c = pltpu.make_async_copy(src, dst, load_sem.at[i])
        c.start()
        return c

    ld_b = load(b_old, bv, 0)
    ld_a = load(a_old, av, 1)

    barrier = pltpu.get_barrier_semaphore()
    for j in range(1, N_DP):
        pl.semaphore_signal(
            barrier, inc=1, device_id=(me_s, (me_d + j) % N_DP), device_id_type=MESH
        )
    for k in range(1, N_SECTION):
        pl.semaphore_signal(
            barrier, inc=1, device_id=((me_s + k) % N_SECTION, me_d), device_id_type=MESH
        )

    ld_cot = load(cotangent, cot, 2)
    ld_b1 = load(b_first_old, bmv1, 3)
    ld_b2 = load(b_second_old, bmv2, 4)

    def x_copy(w, a, b):
        ax = at(b, a) if w == 0 else at(a, b)
        return pltpu.make_async_copy(
            inputs.at[w, :, pl.ds(pl.multiple_of(ax * LD, LD), LD)],
            xin.at[w, a, b],
            x_sem.at[w, a, b],
        )

    dest = []
    for j in range(OLD_DEV):
        total = jnp.int32(0)
        for l in range(LAYERS):
            total += jnp.where(old_slot[l] == me_s * OLD_DEV + j, new_slot[l] // NEW_DEV, 0)
        dest.append(total)
    src_k, present = [], []
    for s in range(NEW_DEV):
        total, has = jnp.int32(0), jnp.int32(0)
        for l in range(LAYERS):
            hit = new_slot[l] == me_s * NEW_DEV + s
            total += jnp.where(hit, old_slot[l] // OLD_DEV, 0)
            has += jnp.where(hit, 1, 0)
        src_k.append((me_s + N_SECTION - total) % N_SECTION)
        present.append(has > 0)
    send_index = []
    for k in range(N_SECTION):
        d = (me_s + k) % N_SECTION
        pick = jnp.int32(0)
        for j in range(1, OLD_DEV):
            pick = jnp.where(dest[j] == d, j, pick)
        send_index.append(pick)

    receives = me_s < N_NEW

    def peer(k):
        return ((me_s + k) % N_SECTION, me_d)

    def sends_to(k):
        return (me_s + k) % N_SECTION < N_NEW

    def pack_b(v):
        v = v.astype(F32)
        return jnp.concatenate([v[:HALF], v[HALF:]], axis=1).astype(BF16)

    @pl.when(jnp.logical_not(receives))
    def _():
        b_recv[...] = jnp.zeros_like(b_recv)
        bm_recv[...] = jnp.zeros_like(bm_recv)
        a_recv0[...] = jnp.zeros_like(a_recv0)
        a_recv1[...] = jnp.zeros_like(a_recv1)
        m_recv[...] = jnp.zeros_like(m_recv)

    ld_b.wait()
    for k in range(N_SECTION):
        v = pack_b(bv[send_index[k]])
        if k == 0:
            b_recv[0] = v
        else:
            b_stage[k] = v
    b_msgs = {
        k: msgs.make(b_stage.at[k], b_recv.at[k], peer(k)) for k in range(1, N_SECTION)
    }
    pl.semaphore_wait(barrier, N_DP - 1 + N_SECTION - 1)

    def start_all(group):
        for k, m in group.items():
            @pl.when(sends_to(k))
            def _(m=m):
                m.start()

    def recv_all(group):
        @pl.when(receives)
        def _():
            for m in group.values():
                m.wait_recv()

    def wait_sent(group):
        for k, m in group.items():
            @pl.when(sends_to(k))
            def _(m=m):
                m.wait_send()

    start_all(b_msgs)

    ld_a.wait()
    a_stage, a_recv = (a_stage0, a_stage1), (a_recv0, a_recv1)
    a_msgs = []
    for h in range(2):
        for k in range(N_SECTION):
            v = av[send_index[k], pl.ds(h * HALF, HALF), :]
            if k == 0:
                a_recv[h][0] = v
            else:
                a_stage[h][k] = v
        group = {
            k: msgs.make(a_stage[h].at[k], a_recv[h].at[k], peer(k))
            for k in range(1, N_SECTION)
        }
        start_all(group)
        a_msgs.append(group)

    for w in range(WIN):
        for b in range(SIDE):
            for a in range(SIDE):
                x_copy(w, a, b).start()
    ld_m1 = load(a_first_old, mv1, 5)
    ld_m2 = load(a_second_old, mv2, 6)

    recv_all(b_msgs)

    def unpack_b(v):
        v = v.astype(F32)
        return jnp.concatenate([v[:, :LK], v[:, LK:]], axis=0)

    pbs = []
    for s in range(NEW_DEV):
        v = b_recv[src_k[s]]
        v = jnp.where(present[s], v, jnp.zeros_like(v))
        pb[s] = v
        if s < WIN:
            pbs.append(unpack_b(v))
    bfull[me_d] = jnp.concatenate(pbs, axis=1).astype(BF16)
    bg_msgs = []
    for j in range(1, N_DP):
        m = msgs.make(bfull.at[me_d], bfull.at[me_d], (me_s, (me_d + j) % N_DP))
        m.start()
        bg_msgs.append(m)

    def nbr(w, axis, step):
        on_x = (axis == 1) == (w == 0)
        return (me_s, at(step, 0) if on_x else at(0, step))

    ag = {}
    PLUS, MINUS = 1, 3

    def ag_make(w, a, b, h, axis, step):
        na, nb = (a, b)
        if axis == 0:
            na = (a - step) % SIDE
        else:
            nb = (b - step) % SIDE
        rows = pl.ds(h * HALF, HALF)
        m = msgs.make(
            afull.at[w, a, b, rows], afull.at[w, na, nb, rows], nbr(w, axis, step)
        )
        assert (w, na, nb, h) not in ag
        ag[(w, na, nb, h)] = m
        m.start()

    def ag_on(w, a, b, h):
        if b == 0:
            if a == 0:
                ag_make(w, a, b, h, 0, 1)
                ag_make(w, a, b, h, 0, -1)
            elif a == 3 and h == 0:
                ag_make(w, a, b, h, 0, 1)
            elif a == 1 and h == 1:
                ag_make(w, a, b, h, 0, -1)
            ag_make(w, a, b, h, 1, 1)
            ag_make(w, a, b, h, 1, -1)
        elif b == 3 and h == 0:
            ag_make(w, a, b, h, 1, 1)
        elif b == 1 and h == 1:
            ag_make(w, a, b, h, 1, -1)

    for h in range(2):
        recv_all(a_msgs[h])
        rows = pl.ds(h * HALF, HALF)
        for s in range(NEW_DEV):
            v = a_recv[h][src_k[s]]
            v = jnp.where(present[s], v, jnp.zeros_like(v))
            pa[s, rows] = v
            if s < WIN:
                afull[s, 0, 0, rows] = v
                ag_on(s, 0, 0, h)

    ld_b1.wait()
    ld_b2.wait()
    ld_m1.wait()
    ld_m2.wait()
    for k in range(N_SECTION):
        bm = jnp.concatenate([bmv1[send_index[k]], bmv2[send_index[k]]], axis=1).astype(BF16)
        for i, mv in enumerate((mv1, mv2)):
            v = mv[send_index[k]].astype(BF16)
            if k == 0:
                m_recv[0, i] = v
            else:
                m_stage[k, i] = v
        if k == 0:
            bm_recv[0] = bm
        else:
            bm_stage[k] = bm
    bm_msgs = {
        k: msgs.make(bm_stage.at[k], bm_recv.at[k], peer(k)) for k in range(1, N_SECTION)
    }
    m_msgs = {k: msgs.make(m_stage.at[k], m_recv.at[k], peer(k)) for k in range(1, N_SECTION)}
    start_all(bm_msgs)
    start_all(m_msgs)

    for j in range(1, N_DP):
        bg_msgs[j - 1].wait_recv()
    for d in range(0, N_DP, 2):
        lo, hi = bfull[d].astype(F32), bfull[d + 1].astype(F32)
        cols = pl.ds(d * LK, 2 * LK)
        bw[0, :, cols] = jnp.concatenate([lo[:, :LK], hi[:, :LK]], axis=1).astype(BF16)
        bw[1, :, cols] = jnp.concatenate([lo[:, LK:], hi[:, LK:]], axis=1).astype(BF16)
    ld_cot.wait()
    for w in range(WIN):
        pulled[w] = dot_nt(bw[w], cot[w]).astype(BF16)

    for w in range(WIN):
        for b in range(SIDE):
            for a in range(SIDE):
                x_copy(w, a, b).wait()

    def partial(w, f, s):
        return dot_nn(pulled[w], xin[w, s, f])

    lat_acc[...] = jnp.zeros_like(lat_acc)

    def add_latent(w, a, b):
        lat_acc[w] += dot_nt(afull[w, a, b], xin[w, a, b])

    def rs_nbr(w, axis, step):
        on_x = (axis == 0) == (w == 0)
        return (me_s, at(step, 0) if on_x else at(0, step))

    rs = {}

    def rs_send(key, w, i, step):
        m = msgs.make(gsend.at[w, i], grecv.at[w, i], rs_nbr(w, 0, step))
        m.start()
        rs[key] = m

    VIA = {0: 1, 1: 1, 2: -1, 3: -1}

    def rs_m1(w, s):
        gsend[w, s] = partial(w, 2, s).astype(BF16)
        rs_send((w, "m1", s), w, s, VIA[s])

    def rs_m2(w, s):
        f = (-VIA[s]) % SIDE
        gsend[w, 4 + s] = partial(w, f, s).astype(BF16)
        rs_send((w, "m2", s), w, 4 + s, -VIA[s])

    def rs_m3(w, s):
        f = VIA[s] % SIDE
        rs[(w, "m1", s)].wait_recv()
        gsend[w, 8 + s] = (partial(w, f, s) + grecv[w, s].astype(F32)).astype(BF16)
        rs_send((w, "m3", s), w, 8 + s, VIA[s])

    def rs_own(w, s):
        g = partial(w, 0, s)
        rs[(w, "m2", s)].wait_recv()
        rs[(w, "m3", s)].wait_recv()
        return g + grecv[w, 4 + s].astype(F32) + grecv[w, 8 + s].astype(F32)

    def rs2_send(key, w, i, step):
        m = msgs.make(hsend.at[w, i], hrecv.at[w, i], rs_nbr(w, 1, step))
        m.start()
        rs[key] = m

    order = []
    for h in range(2):
        order += [(3, 0, h), (1, 0, h)]
    for h in range(2):
        order += [(0, 3, h), (0, 1, h)]
    order += [(2, 0, 0), (2, 0, 1)]
    for a in (3, 1):
        for h in range(2):
            order += [(a, 3, h), (a, 1, h)]
    order += [(0, 2, 0), (0, 2, 1)]
    for h in range(2):
        order += [(2, 3, h), (2, 1, h)]
    for a in (3, 1, 2):
        order += [(a, 2, 0), (a, 2, 1)]
    todo = [(0, 0)]
    arrived = {}
    for n, (a, b, h) in enumerate(order):
        for w in range(WIN):
            ag[(w, a, b, h)].wait_recv()
            ag_on(w, a, b, h)
        arrived[(a, b)] = arrived.get((a, b), 0) + 1
        if todo:
            ta, tb = todo.pop(0)
            for w in range(WIN):
                add_latent(w, ta, tb)
        if arrived[(a, b)] == 2:
            todo.append((a, b))
        if 14 <= n < 18:
            s = (2, 3, 1, 0)[n - 14]
            for w in range(WIN):
                rs_m1(w, s)
        if 18 <= n < 22:
            s = (2, 3, 1, 0)[n - 18]
            for w in range(WIN):
                rs_m2(w, s)
    for ta, tb in todo:
        for w in range(WIN):
            add_latent(w, ta, tb)

    for w in range(WIN):
        lat[w] = lat_acc[w].astype(BF16)
    g0 = dot_nn(lat[0], cot[0]) * adapter_scale
    g1 = dot_nn(lat[1], cot[1]) * adapter_scale
    for d in range(N_DP):
        cols = slice(d * LK, (d + 1) * LK)
        gb_stage[d] = jnp.concatenate([g0[:, cols], g1[:, cols]], axis=1).astype(BF16)
    gb_recv[0] = gb_stage[me_d]
    gb_msgs = []
    for j in range(1, N_DP):
        to = (me_d + j) % N_DP
        m = msgs.make(gb_stage.at[to], gb_recv.at[j], (me_s, to))
        m.start()
        gb_msgs.append(m)

    for s in (2, 3, 1, 0):
        for w in range(WIN):
            rs_m3(w, s)

    outs = []

    def put(src, dst, i):
        c = pltpu.make_async_copy(src, dst, out_sem.at[i])
        c.start()
        outs.append(c)

    put(pa, pa_out, 0)
    put(pb, pb_out, 1)
    put(lat, lat_out, 2)
    put(bw, bw_out, 3)
    recv_all(bm_msgs)
    recv_all(m_msgs)
    for s in range(NEW_DEV):
        v = bm_recv[src_k[s]]
        pbm[s] = jnp.where(present[s], v, jnp.zeros_like(v))
        for i in range(2):
            v = m_recv[src_k[s], i]
            pm[s, i] = jnp.where(present[s], v, jnp.zeros_like(v))
    put(pbm, pbm_out, 4)
    put(pm, pm_out, 5)

    top, bottom = pl.ds(0, HALF), pl.ds(HALF, HALF)
    for w in range(WIN):
        g = rs_own(w, 2)
        hsend[w, 0] = g[:HALF].astype(BF16)
        rs2_send((w, "n1", 1), w, 0, 1)
        hsend[w, 1] = g[HALF:].astype(BF16)
        rs2_send((w, "n1", 3), w, 1, -1)
    for w in range(WIN):
        g = rs_own(w, 3)
        hsend[w, 2] = g[:HALF].astype(BF16)
        rs2_send((w, "n2", 3), w, 2, -1)
        hbuf[w, 0] = g[HALF:]
        g = rs_own(w, 1)
        hsend[w, 3] = g[HALF:].astype(BF16)
        rs2_send((w, "n2", 1), w, 3, 1)
        hbuf[w, 1] = g[:HALF]
    for w in range(WIN):
        rs[(w, "n1", 1)].wait_recv()
        hsend[w, 4] = (hbuf[w, 1] + hrecv[w, 0].astype(F32)).astype(BF16)
        rs2_send((w, "n3", 1), w, 4, 1)
        rs[(w, "n1", 3)].wait_recv()
        hsend[w, 5] = (hbuf[w, 0] + hrecv[w, 1].astype(F32)).astype(BF16)
        rs2_send((w, "n3", 3), w, 5, -1)
    for w in range(WIN):
        ga[w] = rs_own(w, 0)

    for m in gb_msgs:
        m.wait_recv()
    total = gb_recv[0].astype(F32)
    for j in range(1, N_DP):
        total += gb_recv[j].astype(F32)
    gb[...] = total
    put(gb, gb_out, 6)

    for w in range(WIN):
        rs[(w, "n2", 3)].wait_recv()
        rs[(w, "n3", 1)].wait_recv()
        ga[w, top] = adapter_scale * (
            ga[w, top] + hrecv[w, 2].astype(F32) + hrecv[w, 4].astype(F32)
        )
        rs[(w, "n2", 1)].wait_recv()
        rs[(w, "n3", 3)].wait_recv()
        ga[w, bottom] = adapter_scale * (
            ga[w, bottom] + hrecv[w, 3].astype(F32) + hrecv[w, 5].astype(F32)
        )
    put(ga, ga_out, 7)

    for group in (b_msgs, a_msgs[0], a_msgs[1], bm_msgs, m_msgs):
        wait_sent(group)
    for m in bg_msgs + gb_msgs + list(ag.values()) + list(rs.values()):
        m.wait_send()
    for c in outs:
        c.wait()
    assert msgs.count <= N_MSG


def exchange(*args):
    shape = jax.ShapeDtypeStruct
    anywhere = pl.BlockSpec(memory_space=pl.ANY)
    smem = pl.BlockSpec(memory_space=pltpu.SMEM)
    dma = pltpu.SemaphoreType.DMA
    V = pltpu.VMEM
    return pl.pallas_call(
        exchange_kernel,
        out_shape=(
            shape((NEW_DEV, R, LD), BF16),
            shape((NEW_DEV, 2, R, LD), BF16),
            shape((NEW_DEV, HALF, 2 * LK), BF16),
            shape((NEW_DEV, R, 2 * LK), BF16),
            shape((WIN, R, LD), F32),
            shape((R, 2 * LK), F32),
            shape((WIN, R, TOK), BF16),
            shape((WIN, R, KV), BF16),
        ),
        in_specs=[smem, smem] + [anywhere] * 8,
        out_specs=[anywhere] * 8,
        scratch_shapes=[
            V((WIN, SIDE, SIDE, TOK, LD), BF16),
            V((WIN, TOK, KV), BF16),
            V((OLD_DEV, R, LD), BF16),
            V((OLD_DEV, R, LD), F32),
            V((OLD_DEV, R, LD), F32),
            V((OLD_DEV, R, LK), BF16),
            V((OLD_DEV, R, LK), F32),
            V((OLD_DEV, R, LK), F32),
            V((N_SECTION, HALF, 2 * LK), BF16),
            V((N_SECTION, HALF, 2 * LK), BF16),
            V((N_SECTION, R, 2 * LK), BF16),
            V((N_SECTION, R, 2 * LK), BF16),
            V((N_SECTION, HALF, LD), BF16),
            V((N_SECTION, HALF, LD), BF16),
            V((N_SECTION, HALF, LD), BF16),
            V((N_SECTION, HALF, LD), BF16),
            V((N_SECTION, 2, R, LD), BF16),
            V((N_SECTION, 2, R, LD), BF16),
            V((WIN, SIDE, SIDE, R, LD), BF16),
            V((N_DP, R, 2 * LK), BF16),
            V((WIN, R, KV), BF16),
            V((WIN, R, TOK), BF16),
            V((WIN, R, TOK), F32),
            V((WIN, R, TOK), BF16),
            V((N_DP, R, 2 * LK), BF16),
            V((N_DP, R, 2 * LK), BF16),
            V((WIN, 12, R, LD), BF16),
            V((WIN, 12, R, LD), BF16),
            V((WIN, 2, HALF, LD), F32),
            V((WIN, 6, HALF, LD), BF16),
            V((WIN, 6, HALF, LD), BF16),
            V((NEW_DEV, R, LD), BF16),
            V((NEW_DEV, 2, R, LD), BF16),
            V((NEW_DEV, HALF, 2 * LK), BF16),
            V((NEW_DEV, R, 2 * LK), BF16),
            V((WIN, R, LD), F32),
            V((R, 2 * LK), F32),
            dma((N_MSG,)),
            dma((N_MSG,)),
            dma((8,)),
            dma((WIN, SIDE, SIDE)),
            dma((8,)),
        ],
        compiler_params=pltpu.CompilerParams(
            collective_id=0, has_side_effects=True, vmem_limit_bytes=56 * 1024 * 1024
        ),
    )(*args)


def adam(first, second, grad):
    first_new = beta_one * first + (1.0 - beta_one) * grad
    second_new = beta_two * second + (1.0 - beta_two) * grad * grad
    direction = first_new / corr_one / (jnp.sqrt(second_new / corr_two) + adam_eps)
    return first_new, second_new, direction


def finish_kernel(
    pa, pm, pb, pbm, ga, gb, lat, bw, out, new_a, new_b, fa, sa, fb, sb, step_a, step_b
):
    s = pl.program_id(0)
    new_a[...] = pa[...]
    v = pb[0].astype(F32)
    new_b[0] = jnp.concatenate([v[:, :LK], v[:, LK:]], axis=0).astype(BF16)
    first, second = pm[0, 0].astype(F32), pm[0, 1].astype(F32)
    bm = pbm[0].astype(F32)
    first_b, second_b = bm[:, :LK], bm[:, LK:]

    @pl.when(s < WIN)
    def _():
        f, q, d = adam(first, second, ga[0])
        fa[0], sa[0], step_a[0] = f, q, d
        g = gb[...]
        g = jnp.where(s == 0, g[:, :LK], g[:, LK:])
        f, q, d = adam(first_b, second_b, g)
        fb[0], sb[0], step_b[0] = f, q, d
        product = lax.dot_general(
            lat[0], bw[0], (((0,), (0,)), ((), ())), preferred_element_type=F32
        )
        out[0] = (adapter_scale * product).astype(BF16)

    @pl.when(s >= WIN)
    def _():
        fa[0], sa[0] = first, second
        fb[0], sb[0] = first_b, second_b


def finish(*args):
    shape = jax.ShapeDtypeStruct

    def every(*dims):
        return pl.BlockSpec((1,) + dims, lambda s: (s,) + (0,) * len(dims))

    def window(*dims):
        return pl.BlockSpec((1,) + dims, lambda s: (jnp.minimum(s, WIN - 1),) + (0,) * len(dims))

    return pl.pallas_call(
        finish_kernel,
        grid=(NEW_DEV,),
        out_shape=(
            shape((WIN, TOK, KV), BF16),
            shape((NEW_DEV, R, LD), BF16),
            shape((NEW_DEV, R, LK), BF16),
            shape((NEW_DEV, R, LD), F32),
            shape((NEW_DEV, R, LD), F32),
            shape((NEW_DEV, R, LK), F32),
            shape((NEW_DEV, R, LK), F32),
            shape((WIN, R, LD), F32),
            shape((WIN, R, LK), F32),
        ),
        in_specs=[
            every(R, LD),
            every(2, R, LD),
            every(HALF, 2 * LK),
            every(R, 2 * LK),
            window(R, LD),
            pl.BlockSpec((R, 2 * LK), lambda s: (0, 0)),
            window(R, TOK),
            window(R, KV),
        ],
        out_specs=[
            window(TOK, KV),
            every(R, LD),
            every(R, LK),
            every(R, LD),
            every(R, LD),
            every(R, LK),
            every(R, LK),
            window(R, LD),
            window(R, LK),
        ],
    )(*args)


def body(*args):
    return finish(*exchange(*args))


def solution(mesh):
    state = P("section", None, "dp")
    tokens = P("section", "dp", None)
    in_specs = (P(), P()) + (state,) * 6 + (tokens,) * 2
    out_specs = (tokens,) + (state,) * 8
    return jax.shard_map(body, mesh=mesh, in_specs=in_specs, out_specs=out_specs, check_vma=False)
```

time: 235 us -> 84.2 us (0.36)
  waiting for transfers between devices: 107 us -> 0 us
  Pallas kernels: 0 us -> 83.4 us
  blocking collectives: 26.7 us -> 0 us
  matrix products: 25.9 us -> 0 us
  local copies, waits for them, and re-layouts: 25.1 us -> 0 us
  other arithmetic: 24.7 us -> 0 us
  between operations: 14.4 us -> 0.65 us
  starting transfers between devices: 9.33 us -> 0 us
    psum x1 -> x0, waiting for transfers between devices: 90.1 us -> none  [body(): lax.psum((adapter_scale * product_term).reshape(inputs.shape[2], -1).asty...]
    pallas_call x0 -> x2, Pallas kernels: none -> 83.4 us  [the longest x1 78 us: exchange(): pl.pallas_call(exchange_kernel, out_shape=(shape((NEW_DEV, R, LD), BF16),...]
    all_gather x1 -> x0, blocking collectives: 26.7 us -> none  [body(): lax.all_gather(new_b[:WIN], 'dp', axis=2, tiled=True)]
    dot_general x4 -> x0, matrix products: 25.9 us -> none  [the longest x1 12.2 us: body(): jnp.einsum('wtd,wrd->wtr', inputs, full_a, preferred_element_type=jnp.flo...]
    all_to_all x2 -> x0, waiting for transfers between devices: 17.1 us -> none  [the longest x1 17 us: body(): lax.all_to_all(select_rows(factors, send_index, send_has), 'section', spl...]
    gather x4 -> x0, local copies, waits for them, and re-layouts: 13.7 us -> none  [select_rows(): picked = jnp.take(array, index, axis=0)]
    select_n x8 -> x0, other arithmetic: 11.2 us -> none  [the longest x4 10.4 us: select_rows(): return jnp.where(flag.reshape(array_shape), picked, jnp.zeros_like(picked))]
    all_to_all x2 -> x0, starting transfers between devices: 9.25 us -> none  [the longest x1 4.69 us: body(): lax.all_to_all(select_rows(factors, send_index, send_has), 'section', spl...]
  transfers between devices with their start and end apart: 4 -> 0, of which waited for: 2 -> 0; matrix products, arithmetic and copies ran while one was open for 25% -> 0% of each run, Pallas kernels for 0% -> 0%
where the time goes in v1:
time: 84.2 us; the launch traced here: 84 us
  Pallas kernels  83.4 us (99%)
    pallas_call x1, Pallas kernels, exchange(): pl.pallas_call(exchange_kernel, out_shape=(shape((NEW_DEV, R, LD), BF16),...  78 us
    pallas_call x1, Pallas kernels, finish(): pl.pallas_call(finish_kernel, grid=(NEW_DEV,), out_shape=(shape((WIN, TOK...  5.36 us

profile of v1, /device:TPU:0, one launch (start us, length us, event | category | flops | bytes accessed | tf_op | source)
XLA Modules:
  0.0 84.0 jit_solution(1348736825060903127)
XLA Ops:
  0.6 78.0 %shard_map.169 = (bf16[4,64,1024]{2,1,0:T(8,128)(2,1)}, bf16[4,2,64,1024]{3,2,1,0:T(8,128)(2,1)}, bf16[4,32,128]{2,1,0:T(8,128)(2,1)}, bf16[4,64,128]{2,1,0:T(8,...) custom-call(s32[24]{0:T(128)} %old_slot.1, ...), custom_call_target="tpu_custom_call" | custom-call | tf_op jit(solution)/shard_map/pallas_call | solution.py:561
  78.7 5.4 %shard_map.170 = (bf16[2,256,1024]{2,1,0:T(8,128)(2,1)}, bf16[4,64,1024]{2,1,0:T(8,128)(2,1)}, bf16[4,64,64]{2,1,0:T(8,128)(2,1)}, f32[4,64,1024]{2,1,0:T(8,128)...) custom-call(bf16[4,64,1024]{2,1,0:T(8,128)(2,1)} %get-tuple-element., ...), custom_call_target="tpu_custom_call" | custom-call | tf_op jit(solution)/shard_map/pallas_call | solution.py:671

commit v2 on v1

v2 whole, which is shorter than its diff:
```python
import jax
import jax.numpy as jnp
from jax import lax
from jax.experimental import pallas as pl
from jax.experimental.pallas import tpu as pltpu
from jax.sharding import PartitionSpec as P

MESH = pl.DeviceIdType.MESH
F32 = jnp.float32
BF16 = jnp.bfloat16

OLD_DEV = 3
NEW_DEV = 4
WIN = 2
LAYERS = 24
N_SECTION = 8
N_NEW = 6
N_DP = 16
SIDE = 4
R = 64
HALF = 32
CHUNKS = ((0, 16), (16, 48))
TOK = 256
LD = 1024
LK = 64
KV = 1024

adapter_scale = 2.0
beta_one = 0.9
beta_two = 0.999
adam_eps = 1e-08
corr_one = 1.0 - (0.9**10) ** 10
corr_two = 1.0 - (0.999**10) ** 10


def dot_nt(a, b):
    return lax.dot_general(a, b, (((1,), (1,)), ((), ())), preferred_element_type=F32)


def dot_nn(a, b):
    return jnp.dot(a, b, preferred_element_type=F32)


class Messages:
    def __init__(self, send_sem, recv_sem):
        self.send_sem, self.recv_sem = send_sem, recv_sem
        self.count = self.sends = 0

    def make(self, src, dst, device, send=None):
        i = self.count
        self.count += 1
        if send is None:
            send = self.send_sem.at[self.sends]
            self.sends += 1
        return pltpu.make_async_remote_copy(
            src_ref=src,
            dst_ref=dst,
            send_sem=send,
            recv_sem=self.recv_sem.at[i],
            device_id=device,
            device_id_type=MESH,
        )


N_SEND = 47
N_RECV = 143


def exchange_kernel(
    old_slot_hbm,
    new_slot_hbm,
    a_old,
    a_first_old,
    a_second_old,
    b_old,
    b_first_old,
    b_second_old,
    inputs,
    cotangent,
    pa_out,
    pm_out,
    pb_out,
    pbm_out,
    ga_out,
    gb_out,
    lat_out,
    bw_out,
    old_slot,
    new_slot,
    xin,
    cot,
    av,
    mv1,
    mv2,
    bv,
    bmv1,
    bmv2,
    b_stage,
    b_recv,
    bm_stage,
    bm_recv,
    a_stage0,
    a_stage1,
    a_recv0,
    a_recv1,
    m_stage,
    m_recv,
    afull,
    bfull,
    bw,
    pulled,
    lat_acc,
    lat,
    gb_stage,
    gb_recv,
    gb_half,
    gb_last,
    gsend,
    grecv,
    hbuf,
    hsend,
    hrecv,
    pa,
    pm,
    pb,
    pbm,
    ga,
    gb,
    send_sem,
    recv_sem,
    ring_sem,
    load_sem,
    x_sem,
    out_sem,
):
    me_s = lax.axis_index("section")
    me_d = lax.axis_index("dp")
    mx = me_d // SIDE
    mz = me_d % SIDE

    def at(dx, dz):
        return ((mx + dx) % SIDE) * SIDE + (mz + dz) % SIDE

    msgs = Messages(send_sem, recv_sem)

    def load(src, dst, i):
        c = pltpu.make_async_copy(src, dst, load_sem.at[i])
        c.start()
        return c

    row = [(me_s, at(j, 0)) for j in range(1, SIDE)]
    column = [(me_s, at(0, j)) for j in range(1, SIDE)]
    barrier = pltpu.get_barrier_semaphore()
    for k in range(1, N_SECTION):
        pl.semaphore_signal(
            barrier, inc=1, device_id=((me_s + k) % N_SECTION, me_d), device_id_type=MESH
        )
    for device in row + column:
        pl.semaphore_signal(barrier, inc=1, device_id=device, device_id_type=MESH)

    ld_old = load(old_slot_hbm, old_slot, 7)
    ld_new = load(new_slot_hbm, new_slot, 8)
    ld_a = load(a_old, av, 1)
    ld_b = load(b_old, bv, 0)
    ld_cot = load(cotangent, cot, 2)
    ld_b1 = load(b_first_old, bmv1, 3)
    ld_b2 = load(b_second_old, bmv2, 4)

    def x_copy(w, a, b):
        ax = at(b, a) if w == 0 else at(a, b)
        return pltpu.make_async_copy(
            inputs.at[w, :, pl.ds(pl.multiple_of(ax * LD, LD), LD)],
            xin.at[w, a, b],
            x_sem.at[w],
        )

    ld_old.wait()
    ld_new.wait()
    dest = []
    for j in range(OLD_DEV):
        total = jnp.int32(0)
        for l in range(LAYERS):
            total += jnp.where(old_slot[l] == me_s * OLD_DEV + j, new_slot[l] // NEW_DEV, 0)
        dest.append(total)
    src_k, present = [], []
    for s in range(NEW_DEV):
        total, has = jnp.int32(0), jnp.int32(0)
        for l in range(LAYERS):
            hit = new_slot[l] == me_s * NEW_DEV + s
            total += jnp.where(hit, old_slot[l] // OLD_DEV, 0)
            has += jnp.where(hit, 1, 0)
        src_k.append((me_s + N_SECTION - total) % N_SECTION)
        present.append(has > 0)
    send_index = []
    for k in range(N_SECTION):
        d = (me_s + k) % N_SECTION
        pick = jnp.int32(0)
        for j in range(1, OLD_DEV):
            pick = jnp.where(dest[j] == d, j, pick)
        send_index.append(pick)

    receives = me_s < N_NEW

    def peer(k):
        return ((me_s + k) % N_SECTION, me_d)

    def sends_to(k):
        return (me_s + k) % N_SECTION < N_NEW

    def pack_b(v):
        v = v.astype(F32)
        return jnp.concatenate([v[:HALF], v[HALF:]], axis=1).astype(BF16)

    @pl.when(jnp.logical_not(receives))
    def _():
        b_recv[...] = jnp.zeros_like(b_recv)
        bm_recv[...] = jnp.zeros_like(bm_recv)
        a_recv0[...] = jnp.zeros_like(a_recv0)
        a_recv1[...] = jnp.zeros_like(a_recv1)
        m_recv[...] = jnp.zeros_like(m_recv)

    def start_all(group):
        for k, m in group.items():
            @pl.when(sends_to(k))
            def _(m=m):
                m.start()

    def recv_all(group):
        @pl.when(receives)
        def _():
            for m in group.values():
                m.wait_recv()

    def wait_sent(group):
        for k, m in group.items():
            @pl.when(sends_to(k))
            def _(m=m):
                m.wait_send()

    a_stage, a_recv = (a_stage0, a_stage1), (a_recv0, a_recv1)
    a_msgs = [
        {k: msgs.make(a_stage[h].at[k], a_recv[h].at[k], peer(k)) for k in range(1, N_SECTION)}
        for h in range(2)
    ]

    def stage_a(h):
        start, size = CHUNKS[h]
        for k in range(N_SECTION):
            v = av[send_index[k], pl.ds(start, size), :]
            if k == 0:
                a_recv[h][0] = v
            else:
                a_stage[h][k] = v

    ld_a.wait()
    stage_a(0)
    ld_b.wait()
    for k in range(N_SECTION):
        v = pack_b(bv[send_index[k]])
        if k == 0:
            b_recv[0] = v
        else:
            b_stage[k] = v
    b_msgs = {
        k: msgs.make(b_stage.at[k], b_recv.at[k], peer(k)) for k in range(1, N_SECTION)
    }
    pl.semaphore_wait(barrier, N_SECTION - 1 + 2 * (SIDE - 1))
    start_all(b_msgs)
    start_all(a_msgs[0])
    stage_a(1)

    ld_m1 = load(a_first_old, mv1, 5)
    ld_m2 = load(a_second_old, mv2, 6)
    for w in range(WIN):
        for b in range(SIDE):
            for a in range(SIDE):
                x_copy(w, a, b).start()

    def nbr(w, axis, step):
        on_x = (axis == 1) == (w == 0)
        return (me_s, at(step, 0) if on_x else at(0, step))

    ag = {}
    PLUS, MINUS = 1, 3

    def ag_make(w, a, b, h, axis, step):
        na, nb = (a, b)
        if axis == 0:
            na = (a - step) % SIDE
        else:
            nb = (b - step) % SIDE
        rows = pl.ds(*CHUNKS[h])
        m = msgs.make(
            afull.at[w, a * SIDE + b, rows],
            afull.at[w, na * SIDE + nb, rows],
            nbr(w, axis, step),
            ring_sem.at[0, w],
        )
        assert (w, na, nb, h) not in ag
        ag[(w, na, nb, h)] = m
        m.start()

    def ag_on(w, a, b, h):
        if b == 0:
            if a == 0:
                ag_make(w, a, b, h, 0, 1)
                ag_make(w, a, b, h, 0, -1)
            elif a == 3 and h == 0:
                ag_make(w, a, b, h, 0, 1)
            elif a == 1 and h == 1:
                ag_make(w, a, b, h, 0, -1)
            ag_make(w, a, b, h, 1, 1)
            ag_make(w, a, b, h, 1, -1)
        elif b == 3 and h == a % 2:
            ag_make(w, a, b, h, 1, 1)
        elif b == 1 and h != a % 2:
            ag_make(w, a, b, h, 1, -1)

    def ag_own(h):
        rows = pl.ds(*CHUNKS[h])
        for s in range(NEW_DEV):
            v = a_recv[h][src_k[s]]
            v = jnp.where(present[s], v, jnp.zeros_like(v))
            pa[s, rows] = v
            if s < WIN:
                afull[s, 0, rows] = v
                ag_on(s, 0, 0, h)

    order = [(3, 0), (1, 0), (0, 3), (0, 1), (2, 0), (3, 3), (3, 1), (1, 3), (1, 1)]
    order += [(0, 2), (2, 3), (2, 1), (3, 2), (1, 2), (2, 2)]

    def ag_event(a, b, h):
        for w in range(WIN):
            ag[(w, a, b, h)].wait_recv()
            ag_on(w, a, b, h)

    recv_all(b_msgs)

    def unpack_b(v):
        v = v.astype(F32)
        return jnp.concatenate([v[:, :LK], v[:, LK:]], axis=0)

    pbs = []
    for s in range(NEW_DEV):
        v = b_recv[src_k[s]]
        v = jnp.where(present[s], v, jnp.zeros_like(v))
        pb[s] = v
        if s < WIN:
            pbs.append(unpack_b(v))
    bfull[mx, mz] = jnp.concatenate(pbs, axis=1).astype(BF16)
    bz_msgs, bx_msgs = [], []
    for device in column:
        m = msgs.make(bfull.at[mx, mz], bfull.at[mx, mz], device)
        m.start()
        bz_msgs.append(m)


    recv_all(a_msgs[0])
    start_all(a_msgs[1])
    ag_own(0)
    for m in bz_msgs:
        m.wait_recv()
    for device in row:
        m = msgs.make(bfull.at[mx], bfull.at[mx], device)
        m.start()
        bx_msgs.append(m)
    for a, b in order[:4]:
        ag_event(a, b, 0)

    for m in bx_msgs:
        m.wait_recv()
    for d in range(0, N_DP, 2):
        x, z = d // SIDE, d % SIDE
        lo, hi = bfull[x, z].astype(F32), bfull[x, z + 1].astype(F32)
        cols = pl.ds(d * LK, 2 * LK)
        bw[0, :, cols] = jnp.concatenate([lo[:, :LK], hi[:, :LK]], axis=1).astype(BF16)
        bw[1, :, cols] = jnp.concatenate([lo[:, LK:], hi[:, LK:]], axis=1).astype(BF16)
    ld_cot.wait()
    for w in range(WIN):
        pulled[w] = dot_nt(bw[w], cot[w]).astype(BF16)

    for w in range(WIN):
        pltpu.make_async_copy(xin.at[w], xin.at[w], x_sem.at[w]).wait()

    def partial(w, f, s):
        return dot_nn(pulled[w], xin[w, s, f])

    lat_acc[...] = jnp.zeros_like(lat_acc)

    def add_latent(w, a, b):
        lat_acc[w] += dot_nt(afull[w, a * SIDE + b], xin[w, a, b])

    def rs_nbr(w, axis, step):
        on_x = (axis == 0) == (w == 0)
        return (me_s, at(step, 0) if on_x else at(0, step))

    rs = {}

    def rs_send(key, w, i, step):
        m = msgs.make(gsend.at[w, i], grecv.at[w, i], rs_nbr(w, 0, step), ring_sem.at[1, w])
        m.start()
        rs[key] = m

    VIA = {0: 1, 1: 1, 2: -1, 3: -1}

    def rs_compute(w, s):
        gsend[w, s] = partial(w, 2, s).astype(BF16)
        gsend[w, 4 + s] = partial(w, (-VIA[s]) % SIDE, s).astype(BF16)

    def rs_start(s):
        for w in range(WIN):
            rs_send((w, "m1", s), w, s, VIA[s])
        for w in range(WIN):
            rs_send((w, "m2", s), w, 4 + s, -VIA[s])

    def rs_m3(w, s):
        f = VIA[s] % SIDE
        rs[(w, "m1", s)].wait_recv()
        gsend[w, 8 + s] = (partial(w, f, s) + grecv[w, s].astype(F32)).astype(BF16)
        rs_send((w, "m3", s), w, 8 + s, VIA[s])

    def rs_own(w, s):
        g = partial(w, 0, s)
        rs[(w, "m2", s)].wait_recv()
        rs[(w, "m3", s)].wait_recv()
        return g + grecv[w, 4 + s].astype(F32) + grecv[w, 8 + s].astype(F32)

    def rs2_send(key, w, i, step):
        m = msgs.make(hsend.at[w, i], hrecv.at[w, i], rs_nbr(w, 1, step), ring_sem.at[2, w])
        m.start()
        rs[key] = m

    top, bottom = pl.ds(0, HALF), pl.ds(HALF, HALF)

    def rs_n1(w):
        g = rs_own(w, 2)
        hsend[w, 0] = g[:HALF].astype(BF16)
        rs2_send((w, "n1", 1), w, 0, 1)
        hsend[w, 1] = g[HALF:].astype(BF16)
        rs2_send((w, "n1", 3), w, 1, -1)

    def rs_n2(w):
        g = rs_own(w, 3)
        hsend[w, 2] = g[:HALF].astype(BF16)
        rs2_send((w, "n2", 3), w, 2, -1)
        hbuf[w, 0] = g[HALF:]
        g = rs_own(w, 1)
        hsend[w, 3] = g[HALF:].astype(BF16)
        rs2_send((w, "n2", 1), w, 3, 1)
        hbuf[w, 1] = g[:HALF]

    def rs_n3(w):
        rs[(w, "n1", 1)].wait_recv()
        hsend[w, 4] = (hbuf[w, 1] + hrecv[w, 0].astype(F32)).astype(BF16)
        rs2_send((w, "n3", 1), w, 4, 1)
        rs[(w, "n1", 3)].wait_recv()
        hsend[w, 5] = (hbuf[w, 0] + hrecv[w, 1].astype(F32)).astype(BF16)
        rs2_send((w, "n3", 3), w, 5, -1)

    SUMS = (2, 3, 1, 0)
    todo = [(0, 0)]

    def latent_of_next():
        if todo:
            ta, tb = todo.pop(0)
            for w in range(WIN):
                add_latent(w, ta, tb)

    def early(blocks):
        for a, b in blocks:
            ag_event(a, b, 0)

    def late(blocks):
        for a, b in blocks:
            ag_event(a, b, 1)
            todo.append((a, b))

    def rs_first(s):
        for w in range(WIN):
            rs_compute(w, s)
        rs_start(s)

    def rs_add(s):
        for w in range(WIN):
            rs_m3(w, s)

    rs_first(SUMS[0])
    rs_first(SUMS[1])
    recv_all(a_msgs[1])
    ag_own(1)
    early(order[4:9])
    pass
    pass
    late(order[:4])

    ld_b1.wait()
    ld_b2.wait()
    ld_m1.wait()
    ld_m2.wait()
    for k in range(N_SECTION):
        bm = jnp.concatenate([bmv1[send_index[k]], bmv2[send_index[k]]], axis=1).astype(BF16)
        for i, mv in enumerate((mv1, mv2)):
            v = mv[send_index[k]].astype(BF16)
            if k == 0:
                m_recv[0, i] = v
            else:
                m_stage[k, i] = v
        if k == 0:
            bm_recv[0] = bm
        else:
            bm_stage[k] = bm
    bm_msgs = {
        k: msgs.make(bm_stage.at[k], bm_recv.at[k], peer(k)) for k in range(1, N_SECTION)
    }
    m_msgs = {k: msgs.make(m_stage.at[k], m_recv.at[k], peer(k)) for k in range(1, N_SECTION)}
    start_all(bm_msgs)
    start_all(m_msgs)


    early(order[9:])
    rs_add(SUMS[0])
    rs_first(SUMS[2])
    rs_add(SUMS[1])
    late(order[4:9])
    rs_first(SUMS[3])
    for w in range(WIN):
        rs_n1(w)
    rs_add(SUMS[2])
    for _ in range(4):
        latent_of_next()
    late(order[9:12])
    rs_add(SUMS[3])
    for _ in range(3):
        latent_of_next()
    for w in range(WIN):
        rs_n2(w)
    for _ in range(3):
        latent_of_next()
    late(order[12:])
    for w in range(WIN):
        rs_n3(w)
    for ta, tb in todo:
        for w in range(WIN):
            add_latent(w, ta, tb)

    for w in range(WIN):
        lat[w] = lat_acc[w].astype(BF16)
    g0 = dot_nn(lat[0], cot[0]) * adapter_scale
    g1 = dot_nn(lat[1], cot[1]) * adapter_scale
    for d in range(N_DP):
        cols = slice(d * LK, (d + 1) * LK)
        g = jnp.concatenate([g0[:, cols], g1[:, cols]], axis=1).astype(BF16)
        gb_stage[d // SIDE, d % SIDE] = g
    gx_msgs, gz_msgs = [], []
    for j in range(1, SIDE):
        m = msgs.make(gb_stage.at[(mx + j) % SIDE], gb_recv.at[j], row[j - 1])
        m.start()
        gx_msgs.append(m)
    outs = []

    def put(src, dst, i):
        c = pltpu.make_async_copy(src, dst, out_sem.at[i])
        c.start()
        outs.append(c)

    put(pa, pa_out, 0)
    put(pb, pb_out, 1)
    put(lat, lat_out, 2)
    put(bw, bw_out, 3)
    recv_all(bm_msgs)
    recv_all(m_msgs)
    for s in range(NEW_DEV):
        v = bm_recv[src_k[s]]
        pbm[s] = jnp.where(present[s], v, jnp.zeros_like(v))
        for i in range(2):
            v = m_recv[src_k[s], i]
            pm[s, i] = jnp.where(present[s], v, jnp.zeros_like(v))
    put(pbm, pbm_out, 4)
    put(pm, pm_out, 5)

    for m in gx_msgs:
        m.wait_recv()
    total = gb_stage[mx].astype(F32)
    for j in range(1, SIDE):
        total += gb_recv[j].astype(F32)
    gb_half[...] = total.astype(BF16)
    for j in range(1, SIDE):
        m = msgs.make(gb_half.at[(mz + j) % SIDE], gb_last.at[j], column[j - 1])
        m.start()
        gz_msgs.append(m)
    for w in range(WIN):
        ga[w] = rs_own(w, 0)

    for m in gz_msgs:
        m.wait_recv()
    total = gb_half[mz].astype(F32)
    for j in range(1, SIDE):
        total += gb_last[j].astype(F32)
    gb[...] = total
    put(gb, gb_out, 6)

    for w in range(WIN):
        rs[(w, "n2", 3)].wait_recv()
        rs[(w, "n3", 1)].wait_recv()
        ga[w, top] = adapter_scale * (
            ga[w, top] + hrecv[w, 2].astype(F32) + hrecv[w, 4].astype(F32)
        )
        rs[(w, "n2", 1)].wait_recv()
        rs[(w, "n3", 3)].wait_recv()
        ga[w, bottom] = adapter_scale * (
            ga[w, bottom] + hrecv[w, 3].astype(F32) + hrecv[w, 5].astype(F32)
        )
    put(ga, ga_out, 7)

    for group in (b_msgs, a_msgs[0], a_msgs[1], bm_msgs, m_msgs):
        wait_sent(group)
    small = bz_msgs + bx_msgs + gx_msgs + gz_msgs
    for m in small:
        m.wait_send()
    for w in range(WIN):
        for i, ref in enumerate((afull.at[w, pl.ds(0, N_DP - 1)], gsend.at[w], hsend.at[w])):
            pltpu.make_async_remote_copy(
                src_ref=ref,
                dst_ref=ref,
                send_sem=ring_sem.at[i, w],
                recv_sem=recv_sem.at[0],
                device_id=row[0],
                device_id_type=MESH,
            ).wait_send()
    for c in outs:
        c.wait()
    assert (msgs.sends, msgs.count) == (N_SEND, N_RECV)


def exchange(*args):
    shape = jax.ShapeDtypeStruct
    anywhere = pl.BlockSpec(memory_space=pl.ANY)
    dma = pltpu.SemaphoreType.DMA
    V = pltpu.VMEM
    return pl.pallas_call(
        exchange_kernel,
        out_shape=(
            shape((NEW_DEV, R, LD), BF16),
            shape((NEW_DEV, 2, R, LD), BF16),
            shape((NEW_DEV, HALF, 2 * LK), BF16),
            shape((NEW_DEV, R, 2 * LK), BF16),
            shape((WIN, R, LD), F32),
            shape((R, 2 * LK), F32),
            shape((WIN, R, TOK), BF16),
            shape((WIN, R, KV), BF16),
        ),
        in_specs=[anywhere] * 10,
        out_specs=[anywhere] * 8,
        scratch_shapes=[
            pltpu.SMEM((LAYERS,), jnp.int32),
            pltpu.SMEM((LAYERS,), jnp.int32),
            V((WIN, SIDE, SIDE, TOK, LD), BF16),
            V((WIN, TOK, KV), BF16),
            V((OLD_DEV, R, LD), BF16),
            V((OLD_DEV, R, LD), F32),
            V((OLD_DEV, R, LD), F32),
            V((OLD_DEV, R, LK), BF16),
            V((OLD_DEV, R, LK), F32),
            V((OLD_DEV, R, LK), F32),
            V((N_SECTION, HALF, 2 * LK), BF16),
            V((N_SECTION, HALF, 2 * LK), BF16),
            V((N_SECTION, R, 2 * LK), BF16),
            V((N_SECTION, R, 2 * LK), BF16),
            V((N_SECTION, CHUNKS[0][1], LD), BF16),
            V((N_SECTION, CHUNKS[1][1], LD), BF16),
            V((N_SECTION, CHUNKS[0][1], LD), BF16),
            V((N_SECTION, CHUNKS[1][1], LD), BF16),
            V((N_SECTION, 2, R, LD), BF16),
            V((N_SECTION, 2, R, LD), BF16),
            V((WIN, N_DP, R, LD), BF16),
            V((SIDE, SIDE, R, 2 * LK), BF16),
            V((WIN, R, KV), BF16),
            V((WIN, R, TOK), BF16),
            V((WIN, R, TOK), F32),
            V((WIN, R, TOK), BF16),
            V((SIDE, SIDE, R, 2 * LK), BF16),
            V((SIDE, SIDE, R, 2 * LK), BF16),
            V((SIDE, R, 2 * LK), BF16),
            V((SIDE, R, 2 * LK), BF16),
            V((WIN, 12, R, LD), BF16),
            V((WIN, 12, R, LD), BF16),
            V((WIN, 2, HALF, LD), F32),
            V((WIN, 6, HALF, LD), BF16),
            V((WIN, 6, HALF, LD), BF16),
            V((NEW_DEV, R, LD), BF16),
            V((NEW_DEV, 2, R, LD), BF16),
            V((NEW_DEV, HALF, 2 * LK), BF16),
            V((NEW_DEV, R, 2 * LK), BF16),
            V((WIN, R, LD), F32),
            V((R, 2 * LK), F32),
            dma((N_SEND,)),
            dma((N_RECV,)),
            dma((3, WIN)),
            dma((9,)),
            dma((WIN,)),
            dma((8,)),
        ],
        compiler_params=pltpu.CompilerParams(
            collective_id=0, has_side_effects=True, vmem_limit_bytes=56 * 1024 * 1024
        ),
    )(*args)


def adam(first, second, grad):
    first_new = beta_one * first + (1.0 - beta_one) * grad
    second_new = beta_two * second + (1.0 - beta_two) * grad * grad
    size = jnp.sqrt(second_new * (1.0 / corr_two)) + adam_eps
    return first_new, second_new, first_new * (1.0 / corr_one) / size


def finish_kernel(
    pa,
    pm,
    pb,
    pbm,
    ga,
    gb,
    lat,
    bw,
    out,
    new_a,
    new_b,
    fa,
    sa,
    fb,
    sb,
    step_a,
    step_b,
    pa_v,
    pm_v,
    pb_v,
    pbm_v,
    ga_v,
    gb_v,
    lat_v,
    bw_v,
    out_v,
    new_b_v,
    fa_v,
    sa_v,
    fb_v,
    sb_v,
    step_a_v,
    step_b_v,
    in_sem,
    out_sem,
):
    def copy(src, dst, sem):
        c = pltpu.make_async_copy(src, dst, sem)
        c.start()
        return c

    outs = []

    def put(src, dst):
        outs.append(copy(src, dst, out_sem.at[len(outs)]))

    ld_pm = {}
    for i, s in enumerate((2, 3, 0, 1)):
        ld_pm[s] = copy(pm.at[s], pm_v.at[s], in_sem.at[i])
    ld_ga = [copy(ga.at[w], ga_v.at[w], in_sem.at[4 + w]) for w in range(WIN)]
    ld_lat = copy(lat, lat_v, in_sem.at[6])
    ld_bw = copy(bw, bw_v, in_sem.at[7])
    ld_pb = copy(pb, pb_v, in_sem.at[8])
    ld_pbm = copy(pbm, pbm_v, in_sem.at[9])
    ld_gb = copy(gb, gb_v, in_sem.at[10])
    ld_pa = copy(pa, pa_v, in_sem.at[11])

    ld_pa.wait()
    put(pa_v, new_a)
    for s in (2, 3):
        ld_pm[s].wait()
        fa_v[s] = pm_v[s, 0].astype(F32)
        put(fa_v.at[s], fa.at[s])
        sa_v[s] = pm_v[s, 1].astype(F32)
        put(sa_v.at[s], sa.at[s])
    for w in range(WIN):
        ld_pm[w].wait()
        ld_ga[w].wait()
        f, q, d = adam(pm_v[w, 0].astype(F32), pm_v[w, 1].astype(F32), ga_v[w])
        fa_v[w] = f
        put(fa_v.at[w], fa.at[w])
        sa_v[w] = q
        put(sa_v.at[w], sa.at[w])
        step_a_v[w] = d
        put(step_a_v.at[w], step_a.at[w])
    ld_lat.wait()
    ld_bw.wait()
    for w in range(WIN):
        product = lax.dot_general(
            lat_v[w], bw_v[w], (((0,), (0,)), ((), ())), preferred_element_type=F32
        )
        out_v[w] = (adapter_scale * product).astype(BF16)
        put(out_v.at[w], out.at[w])
    ld_pb.wait()
    ld_pbm.wait()
    ld_gb.wait()
    for s in range(NEW_DEV):
        v = pb_v[s].astype(F32)
        new_b_v[s] = jnp.concatenate([v[:, :LK], v[:, LK:]], axis=0).astype(BF16)
        bm = pbm_v[s].astype(F32)
        f, q = bm[:, :LK], bm[:, LK:]
        if s < WIN:
            f, q, step_b_v[s] = adam(f, q, gb_v[:, s * LK : (s + 1) * LK])
        fb_v[s], sb_v[s] = f, q
    put(new_b_v, new_b)
    put(fb_v, fb)
    put(sb_v, sb)
    put(step_b_v, step_b)
    for c in outs:
        c.wait()


def finish(*args):
    shape = jax.ShapeDtypeStruct
    anywhere = pl.BlockSpec(memory_space=pl.ANY)
    V = pltpu.VMEM
    return pl.pallas_call(
        finish_kernel,
        out_shape=(
            shape((WIN, TOK, KV), BF16),
            shape((NEW_DEV, R, LD), BF16),
            shape((NEW_DEV, R, LK), BF16),
            shape((NEW_DEV, R, LD), F32),
            shape((NEW_DEV, R, LD), F32),
            shape((NEW_DEV, R, LK), F32),
            shape((NEW_DEV, R, LK), F32),
            shape((WIN, R, LD), F32),
            shape((WIN, R, LK), F32),
        ),
        in_specs=[anywhere] * 8,
        out_specs=[anywhere] * 9,
        scratch_shapes=[
            V((NEW_DEV, R, LD), BF16),
            V((NEW_DEV, 2, R, LD), BF16),
            V((NEW_DEV, HALF, 2 * LK), BF16),
            V((NEW_DEV, R, 2 * LK), BF16),
            V((WIN, R, LD), F32),
            V((R, 2 * LK), F32),
            V((WIN, R, TOK), BF16),
            V((WIN, R, KV), BF16),
            V((WIN, TOK, KV), BF16),
            V((NEW_DEV, R, LK), BF16),
            V((NEW_DEV, R, LD), F32),
            V((NEW_DEV, R, LD), F32),
            V((NEW_DEV, R, LK), F32),
            V((NEW_DEV, R, LK), F32),
            V((WIN, R, LD), F32),
            V((WIN, R, LK), F32),
            pltpu.SemaphoreType.DMA((12,)),
            pltpu.SemaphoreType.DMA((17,)),
        ],
        compiler_params=pltpu.CompilerParams(vmem_limit_bytes=56 * 1024 * 1024),
    )(*args)


def body(*args):
    return finish(*exchange(*args))


def solution(mesh):
    state = P("section", None, "dp")
    tokens = P("section", "dp", None)
    in_specs = (P(), P()) + (state,) * 6 + (tokens,) * 2
    out_specs = (tokens,) + (state,) * 8
    return jax.shard_map(body, mesh=mesh, in_specs=in_specs, out_specs=out_specs, check_vma=False)
```

time: 84.2 us -> 79.7 us (0.947)
  Pallas kernels: 83.4 us -> 78.9 us
    pallas_call x1, Pallas kernels: 78 us -> 74.8 us  [exchange(): pl.pallas_call(exchange_kernel, out_shape=(shape((NEW_DEV, R, LD), BF16),...]
    pallas_call x1, Pallas kernels: 5.36 us -> 4.02 us  [finish(): pl.pallas_call(finish_kernel, out_shape=(shape((WIN, TOK, KV), BF16), sha...]
where the time goes in v2:
time: 79.7 us; the launch traced here: 79.5 us
  Pallas kernels  78.9 us (99%)
    pallas_call x1, Pallas kernels, exchange(): pl.pallas_call(exchange_kernel, out_shape=(shape((NEW_DEV, R, LD), BF16),...  74.8 us
    pallas_call x1, Pallas kernels, finish(): pl.pallas_call(finish_kernel, out_shape=(shape((WIN, TOK, KV), BF16), sha...  4.02 us

profile of v2, /device:TPU:0, one launch (start us, length us, event | category | flops | bytes accessed | tf_op | source)
XLA Modules:
  0.0 79.5 jit_solution(12991599475840310273)
XLA Ops:
  0.6 74.8 %shard_map.169 = (bf16[4,64,1024]{2,1,0:T(8,128)(2,1)}, bf16[4,2,64,1024]{3,2,1,0:T(8,128)(2,1)}, bf16[4,32,128]{2,1,0:T(8,128)(2,1)}, bf16[4,64,128]{2,1,0:T(8,...) custom-call(s32[24]{0:T(128)} %old_slot_hbm.1, ...), custom_call_target="tpu_custom_call" | custom-call | tf_op jit(solution)/shard_map/pallas_call | solution.py:640
  75.5 4.0 %shard_map.170 = (bf16[2,256,1024]{2,1,0:T(8,128)(2,1)}, bf16[4,64,1024]{2,1,0:T(8,128)(2,1)}, bf16[4,64,64]{2,1,0:T(8,128)(2,1)}, f32[4,64,1024]{2,1,0:T(8,128)...) custom-call(bf16[4,64,1024]{2,1,0:T(8,128)(2,1)} %get-tuple-element., ...), custom_call_target="tpu_custom_call" | custom-call | tf_op jit(solution)/shard_map/pallas_call | solution.py:823

commit v3 on v2

--- a/solution.py
+++ b/solution.py
@@ -46,9 +46,10 @@
         self.send_sem, self.recv_sem = send_sem, recv_sem
         self.count = self.sends = 0
 
-    def make(self, src, dst, device, send=None):
-        i = self.count
-        self.count += 1
+    def make(self, src, dst, device, send=None, receive=None):
+        if receive is None:
+            receive = self.recv_sem.at[self.count]
+            self.count += 1
         if send is None:
             send = self.send_sem.at[self.sends]
             self.sends += 1
@@ -56,14 +57,16 @@
             src_ref=src,
             dst_ref=dst,
             send_sem=send,
-            recv_sem=self.recv_sem.at[i],
+            recv_sem=receive,
             device_id=device,
             device_id_type=MESH,
         )
 
 
-N_SEND = 47
-N_RECV = 143
+SCHEDULE = ("F0", "F1", "own", "E1", "L0", "moments", "E2", "A0", "F2", "A1", "P2", "L1", "F3")
+SCHEDULE += ("N1", "A2", "P5", "L2", "A3", "P4", "N2", "P3", "L3", "N3", "gb", "gc", "place")
+N_SEND = 12
+N_RECV = 108
 
 
 def exchange_kernel(
@@ -129,6 +132,7 @@
     send_sem,
     recv_sem,
     ring_sem,
+    section_sem,
     load_sem,
     x_sem,
     out_sem,
@@ -165,6 +169,8 @@
     ld_cot = load(cotangent, cot, 2)
     ld_b1 = load(b_first_old, bmv1, 3)
     ld_b2 = load(b_second_old, bmv2, 4)
+    ld_m1 = load(a_first_old, mv1, 5)
+    ld_m2 = load(a_second_old, mv2, 6)
 
     def x_copy(w, a, b):
         ax = at(b, a) if w == 0 else at(a, b)
@@ -219,29 +225,41 @@
         a_recv1[...] = jnp.zeros_like(a_recv1)
         m_recv[...] = jnp.zeros_like(m_recv)
 
+    class Group:
+        def __init__(self, i, stage, landing):
+            self.i, self.stage, self.landing = i, stage, landing
+
+        def message(self, k, first, size):
+            return msgs.make(
+                self.stage.at[pl.ds(first, size)],
+                self.landing.at[pl.ds(first, size)],
+                peer(k),
+                section_sem.at[0, self.i],
+                section_sem.at[1, self.i],
+            )
+
     def start_all(group):
-        for k, m in group.items():
+        for k in range(1, N_SECTION):
             @pl.when(sends_to(k))
-            def _(m=m):
-                m.start()
+            def _(k=k):
+                group.message(k, k, 1).start()
 
     def recv_all(group):
         @pl.when(receives)
         def _():
-            for m in group.values():
-                m.wait_recv()
+            group.message(1, 1, N_SECTION - 1).wait_recv()
 
     def wait_sent(group):
-        for k, m in group.items():
-            @pl.when(sends_to(k))
-            def _(m=m):
-                m.wait_send()
+        @pl.when(receives)
+        def _():
+            group.message(1, 1, N_NEW - 1).wait_send()
+
+        @pl.when(jnp.logical_not(receives))
+        def _():
+            group.message(1, 1, N_NEW).wait_send()
 
     a_stage, a_recv = (a_stage0, a_stage1), (a_recv0, a_recv1)
-    a_msgs = [
-        {k: msgs.make(a_stage[h].at[k], a_recv[h].at[k], peer(k)) for k in range(1, N_SECTION)}
-        for h in range(2)
-    ]
+    a_msgs = [Group(h, a_stage[h], a_recv[h]) for h in range(2)]
 
     def stage_a(h):
         start, size = CHUNKS[h]
@@ -261,20 +279,35 @@
             b_recv[0] = v
         else:
             b_stage[k] = v
-    b_msgs = {
-        k: msgs.make(b_stage.at[k], b_recv.at[k], peer(k)) for k in range(1, N_SECTION)
-    }
+    b_msgs = Group(2, b_stage, b_recv)
     pl.semaphore_wait(barrier, N_SECTION - 1 + 2 * (SIDE - 1))
     start_all(b_msgs)
     start_all(a_msgs[0])
     stage_a(1)
 
-    ld_m1 = load(a_first_old, mv1, 5)
-    ld_m2 = load(a_second_old, mv2, 6)
     for w in range(WIN):
         for b in range(SIDE):
             for a in range(SIDE):
                 x_copy(w, a, b).start()
+
+    ld_b1.wait()
+    ld_b2.wait()
+    ld_m1.wait()
+    ld_m2.wait()
+    for k in range(N_SECTION):
+        bm = jnp.concatenate([bmv1[send_index[k]], bmv2[send_index[k]]], axis=1).astype(BF16)
+        for i, mv in enumerate((mv1, mv2)):
+            v = mv[send_index[k]].astype(BF16)
+            if k == 0:
+                m_recv[0, i] = v
+            else:
+                m_stage[k, i] = v
+        if k == 0:
+            bm_recv[0] = bm
+        else:
+            bm_stage[k] = bm
+    bm_msgs = Group(3, bm_stage, bm_recv)
+    m_msgs = Group(4, m_stage, m_recv)
 
     def nbr(w, axis, step):
         on_x = (axis == 1) == (w == 0)
@@ -484,113 +517,96 @@
         for w in range(WIN):
             rs_m3(w, s)
 
-    rs_first(SUMS[0])
-    rs_first(SUMS[1])
-    recv_all(a_msgs[1])
-    ag_own(1)
-    early(order[4:9])
-    pass
-    pass
-    late(order[:4])
-
-    ld_b1.wait()
-    ld_b2.wait()
-    ld_m1.wait()
-    ld_m2.wait()
-    for k in range(N_SECTION):
-        bm = jnp.concatenate([bmv1[send_index[k]], bmv2[send_index[k]]], axis=1).astype(BF16)
-        for i, mv in enumerate((mv1, mv2)):
-            v = mv[send_index[k]].astype(BF16)
-            if k == 0:
-                m_recv[0, i] = v
-            else:
-                m_stage[k, i] = v
-        if k == 0:
-            bm_recv[0] = bm
-        else:
-            bm_stage[k] = bm
-    bm_msgs = {
-        k: msgs.make(bm_stage.at[k], bm_recv.at[k], peer(k)) for k in range(1, N_SECTION)
-    }
-    m_msgs = {k: msgs.make(m_stage.at[k], m_recv.at[k], peer(k)) for k in range(1, N_SECTION)}
-    start_all(bm_msgs)
-    start_all(m_msgs)
-
-
-    early(order[9:])
-    rs_add(SUMS[0])
-    rs_first(SUMS[2])
-    rs_add(SUMS[1])
-    late(order[4:9])
-    rs_first(SUMS[3])
-    for w in range(WIN):
-        rs_n1(w)
-    rs_add(SUMS[2])
-    for _ in range(4):
-        latent_of_next()
-    late(order[9:12])
-    rs_add(SUMS[3])
-    for _ in range(3):
-        latent_of_next()
-    for w in range(WIN):
-        rs_n2(w)
-    for _ in range(3):
-        latent_of_next()
-    late(order[12:])
-    for w in range(WIN):
-        rs_n3(w)
-    for ta, tb in todo:
+    gx_msgs, gz_msgs, outs = [], [], []
+
+    def gb_rows():
+        while todo:
+            latent_of_next()
         for w in range(WIN):
-            add_latent(w, ta, tb)
-
-    for w in range(WIN):
-        lat[w] = lat_acc[w].astype(BF16)
-    g0 = dot_nn(lat[0], cot[0]) * adapter_scale
-    g1 = dot_nn(lat[1], cot[1]) * adapter_scale
-    for d in range(N_DP):
-        cols = slice(d * LK, (d + 1) * LK)
-        g = jnp.concatenate([g0[:, cols], g1[:, cols]], axis=1).astype(BF16)
-        gb_stage[d // SIDE, d % SIDE] = g
-    gx_msgs, gz_msgs = [], []
-    for j in range(1, SIDE):
-        m = msgs.make(gb_stage.at[(mx + j) % SIDE], gb_recv.at[j], row[j - 1])
-        m.start()
-        gx_msgs.append(m)
-    outs = []
+            lat[w] = lat_acc[w].astype(BF16)
+        g0 = dot_nn(lat[0], cot[0]) * adapter_scale
+        g1 = dot_nn(lat[1], cot[1]) * adapter_scale
+        for d in range(N_DP):
+            cols = slice(d * LK, (d + 1) * LK)
+            g = jnp.concatenate([g0[:, cols], g1[:, cols]], axis=1).astype(BF16)
+            gb_stage[d // SIDE, d % SIDE] = g
+        for j in range(1, SIDE):
+            m = msgs.make(gb_stage.at[(mx + j) % SIDE], gb_recv.at[j], row[j - 1])
+            m.start()
+            gx_msgs.append(m)
+
+    def gb_columns():
+        for m in gx_msgs:
+            m.wait_recv()
+        total = gb_stage[mx].astype(F32)
+        for j in range(1, SIDE):
+            total += gb_recv[j].astype(F32)
+        gb_half[...] = total.astype(BF16)
+        for j in range(1, SIDE):
+            m = msgs.make(gb_half.at[(mz + j) % SIDE], gb_last.at[j], column[j - 1])
+            m.start()
+            gz_msgs.append(m)
 
     def put(src, dst, i):
         c = pltpu.make_async_copy(src, dst, out_sem.at[i])
         c.start()
         outs.append(c)
 
-    put(pa, pa_out, 0)
-    put(pb, pb_out, 1)
+    def place_moments():
+        recv_all(bm_msgs)
+        recv_all(m_msgs)
+        for s in range(NEW_DEV):
+            v = bm_recv[src_k[s]]
+            pbm[s] = jnp.where(present[s], v, jnp.zeros_like(v))
+            for i in range(2):
+                v = m_recv[src_k[s], i]
+                pm[s, i] = jnp.where(present[s], v, jnp.zeros_like(v))
+        put(pa, pa_out, 0)
+        put(pb, pb_out, 1)
+        put(pbm, pbm_out, 4)
+        put(pm, pm_out, 5)
+
+    def own_late():
+        recv_all(a_msgs[1])
+        ag_own(1)
+
+    def send_moments():
+        start_all(bm_msgs)
+        start_all(m_msgs)
+
+    def both(step):
+        for w in range(WIN):
+            step(w)
+
+    steps = {
+        "own": own_late,
+        "moments": send_moments,
+        "E1": lambda: early(order[4:9]),
+        "E2": lambda: early(order[9:]),
+        "L0": lambda: late(order[:4]),
+        "L1": lambda: late(order[4:9]),
+        "L2": lambda: late(order[9:12]),
+        "L3": lambda: late(order[12:]),
+        "N1": lambda: both(rs_n1),
+        "N2": lambda: both(rs_n2),
+        "N3": lambda: both(rs_n3),
+        "gb": gb_rows,
+        "gc": gb_columns,
+        "place": place_moments,
+    }
+    for i in range(SIDE):
+        steps[f"F{i}"] = lambda i=i: rs_first(SUMS[i])
+        steps[f"A{i}"] = lambda i=i: rs_add(SUMS[i])
+    for step in SCHEDULE:
+        if step[0] == "P":
+            for _ in range(int(step[1:])):
+                latent_of_next()
+        else:
+            steps[step]()
     put(lat, lat_out, 2)
     put(bw, bw_out, 3)
-    recv_all(bm_msgs)
-    recv_all(m_msgs)
-    for s in range(NEW_DEV):
-        v = bm_recv[src_k[s]]
-        pbm[s] = jnp.where(present[s], v, jnp.zeros_like(v))
-        for i in range(2):
-            v = m_recv[src_k[s], i]
-            pm[s, i] = jnp.where(present[s], v, jnp.zeros_like(v))
-    put(pbm, pbm_out, 4)
-    put(pm, pm_out, 5)
-
-    for m in gx_msgs:
-        m.wait_recv()
-    total = gb_stage[mx].astype(F32)
-    for j in range(1, SIDE):
-        total += gb_recv[j].astype(F32)
-    gb_half[...] = total.astype(BF16)
-    for j in range(1, SIDE):
-        m = msgs.make(gb_half.at[(mz + j) % SIDE], gb_last.at[j], column[j - 1])
-        m.start()
-        gz_msgs.append(m)
     for w in range(WIN):
         ga[w] = rs_own(w, 0)
-
     for m in gz_msgs:
         m.wait_recv()
     total = gb_half[mz].astype(F32)
@@ -696,6 +712,7 @@
             dma((N_SEND,)),
             dma((N_RECV,)),
             dma((3, WIN)),
+            dma((2, 5)),
             dma((9,)),
             dma((WIN,)),
             dma((8,)),

time: 79.7 us -> 78.4 us (0.984)
  Pallas kernels: 78.9 us -> 77.6 us
    pallas_call x1, Pallas kernels: 74.8 us -> 73.6 us  [exchange(): pl.pallas_call(exchange_kernel, out_shape=(shape((NEW_DEV, R, LD), BF16),...]
where the time goes in v3:
time: 78.4 us; the launch traced here: 78.2 us
  Pallas kernels  77.6 us (99%)
    pallas_call x1, Pallas kernels, exchange(): pl.pallas_call(exchange_kernel, out_shape=(shape((NEW_DEV, R, LD), BF16),...  73.6 us
    pallas_call x1, Pallas kernels, finish(): pl.pallas_call(finish_kernel, out_shape=(shape((WIN, TOK, KV), BF16), sha...  4.02 us

profile of v3, /device:TPU:0, one launch (start us, length us, event | category | flops | bytes accessed | tf_op | source)
XLA Modules:
  0.0 78.2 jit_solution(17137542243588697083)
XLA Ops:
  0.6 73.6 %shard_map.169 = (bf16[4,64,1024]{2,1,0:T(8,128)(2,1)}, bf16[4,2,64,1024]{3,2,1,0:T(8,128)(2,1)}, bf16[4,32,128]{2,1,0:T(8,128)(2,1)}, bf16[4,64,128]{2,1,0:T(8,...) custom-call(s32[24]{0:T(128)} %old_slot_hbm.1, ...), custom_call_target="tpu_custom_call" | custom-call | tf_op jit(solution)/shard_map/pallas_call | solution.py:656
  74.2 4.0 %shard_map.170 = (bf16[2,256,1024]{2,1,0:T(8,128)(2,1)}, bf16[4,64,1024]{2,1,0:T(8,128)(2,1)}, bf16[4,64,64]{2,1,0:T(8,128)(2,1)}, f32[4,64,1024]{2,1,0:T(8,128)...) custom-call(bf16[4,64,1024]{2,1,0:T(8,128)(2,1)} %get-tuple-element., ...), custom_call_target="tpu_custom_call" | custom-call | tf_op jit(solution)/shard_map/pallas_call | solution.py:840

commit v4 on v3

--- a/solution.py
+++ b/solution.py
@@ -42,17 +42,14 @@
 
 
 class Messages:
-    def __init__(self, send_sem, recv_sem):
-        self.send_sem, self.recv_sem = send_sem, recv_sem
-        self.count = self.sends = 0
-
-    def make(self, src, dst, device, send=None, receive=None):
+    def __init__(self, recv_sem):
+        self.recv_sem = recv_sem
+        self.count = 0
+
+    def make(self, src, dst, device, send, receive=None):
         if receive is None:
             receive = self.recv_sem.at[self.count]
             self.count += 1
-        if send is None:
-            send = self.send_sem.at[self.sends]
-            self.sends += 1
         return pltpu.make_async_remote_copy(
             src_ref=src,
             dst_ref=dst,
@@ -63,9 +60,8 @@
         )
 
 
-SCHEDULE = ("F0", "F1", "own", "E1", "L0", "moments", "E2", "A0", "F2", "A1", "P2", "L1", "F3")
+SCHEDULE = ("F0", "F1", "own", "E1", "L0", "moments", "E2", "A0", "F2", "P2", "L1", "A1", "F3")
 SCHEDULE += ("N1", "A2", "P5", "L2", "A3", "P4", "N2", "P3", "L3", "N3", "gb", "gc", "place")
-N_SEND = 12
 N_RECV = 108
 
 
@@ -145,7 +141,7 @@
     def at(dx, dz):
         return ((mx + dx) % SIDE) * SIDE + (mz + dz) % SIDE
 
-    msgs = Messages(send_sem, recv_sem)
+    msgs = Messages(recv_sem)
 
     def load(src, dst, i):
         c = pltpu.make_async_copy(src, dst, load_sem.at[i])
@@ -383,7 +379,7 @@
     bfull[mx, mz] = jnp.concatenate(pbs, axis=1).astype(BF16)
     bz_msgs, bx_msgs = [], []
     for device in column:
-        m = msgs.make(bfull.at[mx, mz], bfull.at[mx, mz], device)
+        m = msgs.make(bfull.at[mx, mz], bfull.at[mx, mz], device, send_sem.at[0])
         m.start()
         bz_msgs.append(m)
 
@@ -394,7 +390,7 @@
     for m in bz_msgs:
         m.wait_recv()
     for device in row:
-        m = msgs.make(bfull.at[mx], bfull.at[mx], device)
+        m = msgs.make(bfull.at[mx], bfull.at[mx], device, send_sem.at[1])
         m.start()
         bx_msgs.append(m)
     for a, b in order[:4]:
@@ -531,7 +527,9 @@
             g = jnp.concatenate([g0[:, cols], g1[:, cols]], axis=1).astype(BF16)
             gb_stage[d // SIDE, d % SIDE] = g
         for j in range(1, SIDE):
-            m = msgs.make(gb_stage.at[(mx + j) % SIDE], gb_recv.at[j], row[j - 1])
+            m = msgs.make(
+                gb_stage.at[(mx + j) % SIDE], gb_recv.at[j], row[j - 1], send_sem.at[2]
+            )
             m.start()
             gx_msgs.append(m)
 
@@ -543,7 +541,9 @@
             total += gb_recv[j].astype(F32)
         gb_half[...] = total.astype(BF16)
         for j in range(1, SIDE):
-            m = msgs.make(gb_half.at[(mz + j) % SIDE], gb_last.at[j], column[j - 1])
+            m = msgs.make(
+                gb_half.at[(mz + j) % SIDE], gb_last.at[j], column[j - 1], send_sem.at[3]
+            )
             m.start()
             gz_msgs.append(m)
 
@@ -630,9 +630,10 @@
 
     for group in (b_msgs, a_msgs[0], a_msgs[1], bm_msgs, m_msgs):
         wait_sent(group)
-    small = bz_msgs + bx_msgs + gx_msgs + gz_msgs
-    for m in small:
-        m.wait_send()
+    three = pl.ds(0, SIDE - 1)
+    sent = [bfull.at[0, three], bfull.at[three], gb_stage.at[three], gb_half.at[three]]
+    for i, ref in enumerate(sent):
+        msgs.make(ref, ref, row[0], send_sem.at[i], recv_sem.at[0]).wait_send()
     for w in range(WIN):
         for i, ref in enumerate((afull.at[w, pl.ds(0, N_DP - 1)], gsend.at[w], hsend.at[w])):
             pltpu.make_async_remote_copy(
@@ -645,7 +646,7 @@
             ).wait_send()
     for c in outs:
         c.wait()
-    assert (msgs.sends, msgs.count) == (N_SEND, N_RECV)
+    assert msgs.count == N_RECV
 
 
 def exchange(*args):
@@ -709,7 +710,7 @@
             V((NEW_DEV, R, 2 * LK), BF16),
             V((WIN, R, LD), F32),
             V((R, 2 * LK), F32),
-            dma((N_SEND,)),
+            dma((4,)),
             dma((N_RECV,)),
             dma((3, WIN)),
             dma((2, 5)),

time: 78.4 us -> 78.3 us (level)
  no operation moved by 1% of the time
where the time goes in v4:
time: 78.3 us; the launch traced here: 78.2 us
  Pallas kernels  77.5 us (99%)
    pallas_call x1, Pallas kernels, exchange(): pl.pallas_call(exchange_kernel, out_shape=(shape((NEW_DEV, R, LD), BF16),...  73.5 us
    pallas_call x1, Pallas kernels, finish(): pl.pallas_call(finish_kernel, out_shape=(shape((WIN, TOK, KV), BF16), sha...  4.02 us

profile of v4, /device:TPU:0, one launch (start us, length us, event | category | flops | bytes accessed | tf_op | source)
XLA Modules:
  0.0 78.2 jit_solution(15641692402036420770)
XLA Ops:
  0.6 73.5 %shard_map.169 = (bf16[4,64,1024]{2,1,0:T(8,128)(2,1)}, bf16[4,2,64,1024]{3,2,1,0:T(8,128)(2,1)}, bf16[4,32,128]{2,1,0:T(8,128)(2,1)}, bf16[4,64,128]{2,1,0:T(8,...) custom-call(s32[24]{0:T(128)} %old_slot_hbm.1, ...), custom_call_target="tpu_custom_call" | custom-call | tf_op jit(solution)/shard_map/pallas_call | solution.py:657
  74.1 4.0 %shard_map.170 = (bf16[2,256,1024]{2,1,0:T(8,128)(2,1)}, bf16[4,64,1024]{2,1,0:T(8,128)(2,1)}, bf16[4,64,64]{2,1,0:T(8,128)(2,1)}, f32[4,64,1024]{2,1,0:T(8,128)...) custom-call(bf16[4,64,1024]{2,1,0:T(8,128)(2,1)} %get-tuple-element., ...), custom_call_target="tpu_custom_call" | custom-call | tf_op jit(solution)/shard_map/pallas_call | solution.py:841
